TPU v7x, 32 devices: a whole 2x2x4 slice. The times are simulated.
32 devices in a mesh: level: 4 (over y, x), gx: 4 (over z), gy: 2 (over core).
Axes of the slice: x: 2, y: 2, z: 4, core: 2. Of those that a mesh axis runs over, the one named last changes fastest.
Arguments:
- state: float32 [5, 32, 32, 128], P(None, 'gx', 'gy'), may hold values from -0.75 to 5.3, as said below
Outputs:
- level_states: float32 [4, 5, 32, 32, 128], P('level', None, 'gx', 'gy')
Inputs may be any that keep to these rules, and one draw needn't show every extreme that they name: state[0] is a density from 1.5 to 3; state[1:4] are the density times velocity components, each velocity component of magnitude at most 0.25; state[4] is the total energy, a pressure from 1 to 2 divided by 0.4 plus the kinetic energy.
All inputs are finite; a program needn't handle non-finite values.
Results may differ from a plain program's by a relative error of at most 0.0001.
Values sent between devices are 32-bit elements; how exact they have to be, the bound alone decides.
No kernel may reach another device: no remote copies, remote signals or barrier semaphores. Data moves between devices by JAX's collectives and lax.ppermute only.
A program may use at most 64 MiB of HBM per device.

v0:
```python
import functools

import jax
import jax.numpy as jnp
import ml_dtypes
import numpy as np
from jax import lax
from jax.experimental import pallas as pl
from jax.experimental.pallas import tpu as pltpu
from jax.sharding import PartitionSpec as P

STEPS = 3


DT = 0.1
GAMMA = 1.4
SHEAR_COEFFICIENT = 0.1
CONDUCTIVITY = 0.1
FIRST_COEF = (4.0 / 5.0, -1.0 / 5.0, 4.0 / 105.0, -1.0 / 280.0)
SECOND_CENTER = -205.0 / 72.0
SECOND_COEF = (8.0 / 5.0, -1.0 / 5.0, 8.0 / 315.0, -1.0 / 560.0)
REACH = 4
SCALE = 5040
FIRST_WHOLE = tuple(round(w * SCALE) for w in FIRST_COEF)
SECOND_WHOLE = tuple(round(w * SCALE) for w in SECOND_COEF)
VMEM_BUDGET = 56 * 1024 * 1024


def circulants(extent):
    first = np.zeros((extent, extent), np.float32)
    second = np.zeros((extent, extent), np.float32)
    for place in range(extent):
        for k in range(1, REACH + 1):
            first[place, (place + k) % extent] -= FIRST_WHOLE[k - 1]
            first[place, (place - k) % extent] += FIRST_WHOLE[k - 1]
            second[place, (place + k) % extent] += SECOND_WHOLE[k - 1]
            second[place, (place - k) % extent] += SECOND_WHOLE[k - 1]
    return first, second


def split(value):
    high = value.astype(jnp.bfloat16)
    low = (value - high.astype(jnp.float32)).astype(jnp.bfloat16)
    return high, low


def levels_kernel(rows, where, *refs):
    n_pieces = (len(refs) - 4 - 16) // 2
    mine, theirs = refs[:n_pieces], refs[n_pieces : 2 * n_pieces]
    wz_first, wz_second, wy, out = refs[2 * n_pieces : 2 * n_pieces + 4]
    base, fx, vis, part, G0, A1, A2, B1, A3, B2, C1, B3, C2, D1, C3, D2 = refs[2 * n_pieces + 4 :]
    fields, X, Y, Z = base.shape
    half = mine[0].shape[2]
    level, side = where[0], where[1]
    own = (X - rows) // 2

    starts = []
    place = own
    for piece in range(n_pieces):
        starts.append((own + piece * rows) % X)
    for group, core in ((mine, side), (theirs, 1 - side)):
        at = pl.multiple_of(core * half, half)
        for start, ref in zip(starts, group):
            fit = min(rows, X - start)
            base[:, start : start + fit, pl.ds(at, half), :] = ref[:, :fit]
            if fit < rows:
                base[:, : rows - fit, pl.ds(at, half), :] = ref[:, fit:]

    def pointwise(u):
        rho, m0, m1, m2, energy = u
        inverse = 1.0 / rho
        v0, v1, v2 = m0 * inverse, m1 * inverse, m2 * inverse
        m00, m11, m22 = m0 * v0, m1 * v1, m2 * v2
        m01, m02, m12 = m0 * v1, m0 * v2, m1 * v2
        twice = m00 + m11 + m22
        p = (GAMMA - 1.0) * energy - (0.5 * (GAMMA - 1.0)) * twice
        heat = energy + p
        warm = inverse * ((0.5 * SHEAR_COEFFICIENT) * twice + CONDUCTIVITY * p)
        s = SHEAR_COEFFICIENT
        g = [s * v0, s * v1, s * v2, warm]
        along_x = [m0, m00 + p, m01, m02, heat * v0]
        along_y = [m1, m01, m11 + p, m12, heat * v1]
        along_z = [m2, m02, m12, m22 + p, heat * v2]
        return along_x, along_y, along_z, g

    def flux_rows(make, first, count, whole):
        batch = 2

        def step(i, carry):
            x = first + i * batch
            u = [make(f, x, batch).reshape(batch * Y, Z) for f in range(fields)]
            along_x, along_y, along_z, g = pointwise(u)
            for f in range(fields):
                fx[f, pl.ds(x + REACH, batch)] = along_x[f].reshape(batch, Y, Z)
            for f in range(fields - 1):
                vis[f, pl.ds(x + REACH, batch)] = g[f].reshape(batch, Y, Z)
            if whole:
                gs = [split(v) for v in g]
                zs = [split(v) for v in along_z]
                ys = [split(v) for v in along_y]
                flux = jnp.concatenate([jnp.concatenate(pair, axis=1) for pair in zs], axis=0)
                flux = jnp.dot(flux, wz_first[...], preferred_element_type=jnp.float32)
                soft = jnp.concatenate([jnp.concatenate(pair, axis=1) for pair in gs], axis=0)
                soft = jnp.dot(soft, wz_second[...], preferred_element_type=jnp.float32)
                zero = jnp.zeros((Y, Z), jnp.bfloat16)
                for r in range(batch):
                    cut = slice(r * Y, (r + 1) * Y)
                    columns = []
                    for f in range(fields):
                        pair = [v[cut] for v in gs[f - 1]] if f else [zero, zero]
                        columns.append(jnp.concatenate([v[cut] for v in ys[f]] + pair, axis=0))
                    deep = jnp.dot(wy[...], jnp.concatenate(columns, axis=1), preferred_element_type=jnp.float32)
                    for f in range(fields):
                        total = deep[:, f * Z : (f + 1) * Z]
                        at = f * batch * Y + r * Y
                        total = total + flux[at : at + Y]
                        if f:
                            at = (f - 1) * batch * Y + r * Y
                            total = total + soft[at : at + Y]
                        part[f, x + r] = total
            return carry

        lax.fori_loop(0, count // batch, step, 0)

    def stencil_rows(target, shift, first, count, y_first, y_count):
        block, tile = 8, 8
        across = y_count // tile

        def step(i, carry):
            x = first + (i // across) * block
            y = pl.multiple_of(y_first + (i % across) * tile, tile)
            for f in range(fields):
                flux = fx[f, pl.ds(x, block + 2 * REACH), pl.ds(y, tile), :]
                total = part[f, pl.ds(x, block), pl.ds(y, tile), :]
                if f:
                    g = vis[f - 1, pl.ds(x, block + 2 * REACH), pl.ds(y, tile), :]
                    total = total + (3 * SECOND_CENTER * SCALE) * g[REACH : REACH + block]
                for k in range(1, REACH + 1):
                    ahead = slice(REACH + k, REACH + k + block)
                    behind = slice(REACH - k, REACH - k + block)
                    total = total + float(FIRST_WHOLE[k - 1]) * (flux[behind] - flux[ahead])
                    if f:
                        total = total + float(SECOND_WHOLE[k - 1]) * (g[behind] + g[ahead])
                target[f, pl.ds(x - shift, block), pl.ds(y, tile), :] = (DT / SCALE) * total
            return carry

        lax.fori_loop(0, (count // block) * across, step, 0)

    def tendency(target, make, reach, last=False):
        first, count = own - reach, rows + 2 * reach
        if count >= X:
            first, count = 0, X
            flux_rows(make, 0, X, True)
            for ref in (fx, vis):
                ref[:, :REACH] = ref[:, X : X + REACH]
                ref[:, X + REACH :] = ref[:, REACH : 2 * REACH]
        else:
            flux_rows(make, first, count, True)
            flux_rows(make, first - REACH, REACH, False)
            flux_rows(make, first + count, REACH, False)
        if last:
            stencil_rows(target, first, first, count, side * half, half)
        else:
            stencil_rows(target, first, first, count, 0, Y)

    def rows_of(ref, f, x, n):
        return ref[f, pl.ds(x - (X - ref.shape[1]) // 2, n)]

    def mix(*terms):
        def make(f, x, n):
            total = None
            for weight, ref in terms:
                value = rows_of(ref, f, x, n)
                value = value if weight == 1 else weight * value
                total = value if total is None else total + value
            return total

        return make

    half_step, five, sixth, twelfth = 0.5, 5.0 / 12.0, 1.0 / 6.0, 1.0 / 12.0
    u01 = mix((1, base), (1, G0))
    u02 = mix((1, base), (1, G0), (1, A1))
    u03 = mix((1, base), (1, G0), (1, A1), (1, A2))
    u11 = mix((1, base), (half_step, G0), (half_step, A1))
    u12 = mix((1, base), (five, G0), (sixth, A1), (1, B1), (five, A2))
    u13 = mix((1, base), (five, G0), (twelfth, A1), (1, B1), (twelfth, A2), (1, B2), (five, A3))
    u21 = mix((1, base), (half_step, G0), (half_step, B1))
    u22 = mix((1, base), (five, G0), (sixth, B1), (1, C1), (five, B2))
    u23 = mix((1, base), (five, G0), (twelfth, B1), (1, C1), (twelfth, B2), (1, C2), (five, B3))
    u31 = mix((1, base), (half_step, G0), (half_step, C1))
    u32 = mix((1, base), (five, G0), (sixth, C1), (1, D1), (five, C2))
    u33 = mix((1, base), (five, G0), (twelfth, C1), (1, D1), (twelfth, C2), (1, D2), (five, C3))

    tendency(G0, mix((1, base)), 5 * REACH)
    tendency(A1, u01, 4 * REACH)
    tendency(A2, u02, 3 * REACH)
    tendency(B1, u11, 3 * REACH)
    tendency(A3, u03, 2 * REACH)
    tendency(B2, u12, 2 * REACH)
    tendency(C1, u21, 2 * REACH)
    tendency(B3, u13, REACH)
    tendency(C2, u22, REACH)
    tendency(D1, u31, REACH)
    tendency(C3, u23, 0, last=True)
    tendency(D2, u32, 0, last=True)

    at = pl.multiple_of(side * half, half)
    for p, terms in enumerate(
        (
            ((1, base), (1, G0), (1, A1), (1, A2)),
            ((1, base), (five, G0), (twelfth, A1), (1, B1), (twelfth, A2), (1, B2), (five, A3)),
            ((1, base), (five, G0), (twelfth, B1), (1, C1), (twelfth, B2), (1, C2), (five, B3)),
            ((1, base), (five, G0), (twelfth, C1), (1, D1), (twelfth, C2), (1, D2), (five, C3)),
        )
    ):

        @pl.when(level == p)
        def _():
            for f in range(fields):
                total = None
                for weight, ref in terms:
                    start = own - (X - ref.shape[1]) // 2
                    value = ref[f, start : start + rows, pl.ds(at, half), :]
                    value = value if weight == 1 else weight * value
                    total = value if total is None else total + value
                out[0, f] = total


def run_levels(where, mine, theirs, gx):
    fields, rows, half, Z = mine[0].shape
    X, Y = rows * gx, 2 * half
    first_z, second_z = circulants(Z)
    first_y, second_y = circulants(Y)
    bf16 = ml_dtypes.bfloat16
    wz_first = np.concatenate([first_z.T, first_z.T], axis=0).astype(bf16)
    wz_second = np.concatenate([second_z.T, second_z.T], axis=0).astype(bf16)
    wy = np.concatenate([first_y, first_y, second_y, second_y], axis=1).astype(bf16)

    def hold(n, lead=fields):
        return pltpu.VMEM((lead, n, Y, Z), jnp.float32)

    scratch = [hold(X), hold(X + 2 * REACH), hold(X + 2 * REACH, fields - 1), hold(X)]
    for reach in (5, 4, 3, 3, 2, 2, 2, 1, 1, 1, 0, 0):
        scratch.append(hold(min(X, rows + 2 * reach * REACH)))
    vmem = pl.BlockSpec(memory_space=pltpu.VMEM)
    return pl.pallas_call(
        functools.partial(levels_kernel, rows),
        out_shape=jax.ShapeDtypeStruct((1, fields, rows, half, Z), jnp.float32),
        in_specs=[pl.BlockSpec(memory_space=pltpu.SMEM)] + [vmem] * (2 * gx + 3),
        out_specs=vmem,
        scratch_shapes=scratch,
        compiler_params=pltpu.CompilerParams(vmem_limit_bytes=VMEM_BUDGET),
    )(where, *mine, *theirs, wz_first, wz_second, wy)


def gathered_body(state):
    gx = lax.axis_size("gx")
    where = jnp.stack([lax.axis_index("level"), lax.axis_index("gy")]).astype(jnp.int32)
    mine = [state]
    for ahead in range(1, gx):
        route = [((i + ahead) % gx, i) for i in range(gx)]
        mine.append(lax.ppermute(state, "gx", route))
    theirs = [lax.ppermute(piece, "gy", [(0, 1), (1, 0)]) for piece in mine]
    return run_levels(where, mine, theirs, gx)


def with_halo(block, sides, width):
    for axis, dim in sides:
        count = lax.axis_size(axis)
        forward = [(i, i + 1) for i in range(count - 1)]
        forward.append((count - 1, 0))
        backward = [(target, source) for source, target in forward]
        low = lax.ppermute(
            lax.slice_in_dim(block, block.shape[dim] - width, None, axis=dim), axis, forward
        )
        high = lax.ppermute(lax.slice_in_dim(block, 0, width, axis=dim), axis, backward)
        block = jnp.concatenate([low, block, high], axis=dim)
    return block


def shifted_2(block, axis, distance):
    devices = range(lax.axis_size(axis))
    route = [(i - distance, i) for i in devices if i - distance in devices]
    return lax.ppermute(block, axis, route)


def shifted(quantity, direction, offset):
    extent = quantity.shape[-3:]
    picks = [slice(4, extent[0] - 4), slice(4, extent[1] - 4), slice(4, extent[2] - 4)]
    picks[direction] = slice(4 + offset, extent[direction] - 4 + offset)
    leading = (slice(None),) * (quantity.ndim - 3)
    return quantity[leading + tuple(picks)]


def first_derivative(quantity, direction):
    total = 0.0
    for position, weight in enumerate(FIRST_COEF):
        total = total + weight * (
            shifted(quantity, direction, position + 1) - shifted(quantity, direction, -position - 1)
        )
    return total


def second_derivative_sum(quantity):
    total = 0.0
    for direction in range(3):
        total = total + SECOND_CENTER * shifted(quantity, direction, 0)
        for position, weight in enumerate(SECOND_COEF):
            total = total + weight * (
                shifted(quantity, direction, position + 1)
                + shifted(quantity, direction, -position - 1)
            )
    return total


def tendency(padded):
    specific_volume_inverse = padded[0]
    momentum = padded[1:4]
    energy = padded[4]
    velocity = momentum / specific_volume_inverse
    kinetic_energy_share = 0.5 * jnp.sum(velocity * velocity, axis=0)
    normal_stress_scalar = (GAMMA - 1.0) * (energy - specific_volume_inverse * kinetic_energy_share)
    absolute_kelvin_value = normal_stress_scalar / specific_volume_inverse
    divergence = 0.0
    for direction in range(3):
        along = velocity[direction]
        rows = [
            momentum[component] * along + (normal_stress_scalar if component == direction else 0.0)
            for component in range(3)
        ]
        flux = jnp.stack([momentum[direction]] + rows + [(energy + normal_stress_scalar) * along])
        divergence = divergence + first_derivative(flux, direction)
    viscous = SHEAR_COEFFICIENT * second_derivative_sum(velocity)
    conduction_contribution = SHEAR_COEFFICIENT * second_derivative_sum(
        kinetic_energy_share
    ) + CONDUCTIVITY * second_derivative_sum(absolute_kelvin_value)
    return jnp.concatenate(
        [
            -divergence[0:1],
            viscous - divergence[1:4],
            (conduction_contribution - divergence[4])[None],
        ],
        axis=0,
    )


def wrap_depth(field):
    return jnp.concatenate([field[:, :, :, -4:], field, field[:, :, :, :4]], axis=3)


def padded_faces(field):
    return wrap_depth(with_halo(field, (("gx", 1), ("gy", 2)), 4))


def sections_body(state):
    levels = lax.axis_size("level")
    rank = lax.axis_index("level")
    current = state
    before = jnp.zeros_like(state)
    middle = jnp.zeros_like(state)
    for section in range(STEPS + levels - 1):
        node = section - rank
        forcing = tendency(padded_faces(current))
        newest = shifted_2(forcing, "level", 1)
        quad_term = jnp.where(
            node == 0, 0.5 * (middle + newest), (8.0 * middle + 5.0 * newest - before) / 12.0
        )
        moved = current + DT * (forcing - middle + quad_term)
        active = jnp.logical_and(node >= 0, node < STEPS)
        current = jnp.where(active, moved, current)
        before = middle
        middle = newest
    return current[None]


def body(state):
    fields, rows, half, Z = state.shape
    gx, gy, levels = lax.axis_size("gx"), lax.axis_size("gy"), lax.axis_size("level")
    X, Y = rows * gx, half * gy
    need = 4 * fields * Y * Z * 15 * X
    simple = gy == 2 and levels == 4 and Z == 128 and Y % 32 == 0 and rows == 2 * REACH and half % 16 == 0
    if simple and gx % 2 == 0 and X <= rows + 6 * REACH and need <= VMEM_BUDGET:
        return gathered_body(state)
    return sections_body(state)


def solution(mesh):
    return jax.shard_map(
        body,
        mesh=mesh,
        in_specs=(P(None, "gx", "gy", None),),
        out_specs=P("level", None, "gx", "gy", None),
        check_vma=False,
    )
```

profile of v0, /device:TPU:15, one launch (start us, length us, event | category | flops | bytes accessed | tf_op | source)
XLA Modules:
  0.0 96.3 jit_solution(2834611605549131907)
XLA Ops:
  0.0 1.3 %collective-permute-start.2 = (f32[5,8,16,128]{3,2,1,0:T(8,128)}, f32[5,8,16,128]{3,2,1,0:T(8,128)S(1)}, u32[]{:S(2)}, u32[]{:S(2)}) collective-permute-start(f32[5,8,16,128]{3,2,1,0:T(8,128)} %refs_0_.1), channel_id=1, source_target_pairs={{6,0},{0,2},{2,4},{4,6},{7,1},{1,3},{3,5},{5,7},{14,8},{8,10},{10,... | collective-permute-start | bytes 983048 | tf_op jit(solution)/shard_map/ppermute | solution.py:262
  1.3 1.0 %collective-permute-start.1 = (f32[5,8,16,128]{3,2,1,0:T(8,128)}, f32[5,8,16,128]{3,2,1,0:T(8,128)S(1)}, u32[]{:S(2)}, u32[]{:S(2)}) collective-permute-start(f32[5,8,16,128]{3,2,1,0:T(8,128)} %refs_0_.1), channel_id=1, source_target_pairs={{4,0},{6,2},{0,4},{2,6},{5,1},{7,3},{1,5},{3,7},{12,8},{14,10},{8,... | collective-permute-start | bytes 983048 | tf_op jit(solution)/shard_map/ppermute | solution.py:262
  2.3 1.5 %collective-permute-start = (f32[5,8,16,128]{3,2,1,0:T(8,128)}, f32[5,8,16,128]{3,2,1,0:T(8,128)S(1)}, u32[]{:S(2)}, u32[]{:S(2)}) collective-permute-start(f32[5,8,16,128]{3,2,1,0:T(8,128)} %refs_0_.1), channel_id=1, source_target_pairs={{2,0},{4,2},{6,4},{0,6},{3,1},{5,3},{7,5},{1,7},{10,8},{12,10},{14... | collective-permute-start | bytes 983048 | tf_op jit(solution)/shard_map/ppermute | solution.py:262
  3.8 1.5 %collective-permute-start.3 = (f32[5,8,16,128]{3,2,1,0:T(8,128)}, f32[5,8,16,128]{3,2,1,0:T(8,128)S(1)}, u32[]{:S(2)}, u32[]{:S(2)}) collective-permute-start(f32[5,8,16,128]{3,2,1,0:T(8,128)} %refs_0_.1), channel_id=1, source_target_pairs={{0,1},{1,0},{2,3},{3,2},{4,5},{5,4},{6,7},{7,6},{8,9},{9,8},{10,11... | collective-permute-start | bytes 983048 | tf_op jit(solution)/shard_map/ppermute | solution.py:263
  5.3 3.5 %collective-permute-done.2.refs_3_ = f32[5,8,16,128]{3,2,1,0:T(8,128)S(1)} collective-permute-done((f32[5,8,16,128]{3,2,1,0:T(8,128)}, f32[5,8,16,128]{3,2,1,0:T(8,128)S(1)}, u32[]{:S(2)}, u32[]{:S(2)}) %collective-permute-start.2) | collective-permute-done | bytes 327712 | tf_op jit(solution)/shard_map/ppermute | solution.py:262
  8.8 15.9 %collective-permute-start.6 = (f32[5,8,16,128]{3,2,1,0:T(8,128)S(1)}, f32[5,8,16,128]{3,2,1,0:T(8,128)S(1)}, u32[]{:S(2)}, u32[]{:S(2)}) collective-permute-start(f32[5,8,16,128]{3,2,1,0:T(8,128)S(1)} %collective-permute-done.2.refs_3_), channel_id=1, source_target_pairs={{0,1},{1,0},{2,3},{3,2},{4,5},{5,4},{6,7},{7,6},{8,9},{9,8},{10,11... | collective-permute-start | bytes 983048 | tf_op jit(solution)/shard_map/ppermute | solution.py:263
  24.7 4.3 %collective-permute-done.1.refs_2_ = f32[5,8,16,128]{3,2,1,0:T(8,128)S(1)} collective-permute-done((f32[5,8,16,128]{3,2,1,0:T(8,128)}, f32[5,8,16,128]{3,2,1,0:T(8,128)S(1)}, u32[]{:S(2)}, u32[]{:S(2)}) %collective-permute-start.1) | collective-permute-done | bytes 327712 | tf_op jit(solution)/shard_map/ppermute | solution.py:262
  29.1 1.5 %collective-permute-start.5 = (f32[5,8,16,128]{3,2,1,0:T(8,128)S(1)}, f32[5,8,16,128]{3,2,1,0:T(8,128)S(1)}, u32[]{:S(2)}, u32[]{:S(2)}) collective-permute-start(f32[5,8,16,128]{3,2,1,0:T(8,128)S(1)} %collective-permute-done.1.refs_2_), channel_id=1, source_target_pairs={{0,1},{1,0},{2,3},{3,2},{4,5},{5,4},{6,7},{7,6},{8,9},{9,8},{10,11... | collective-permute-start | bytes 983048 | tf_op jit(solution)/shard_map/ppermute | solution.py:263
  30.6 1.2 %collective-permute-done.refs_1_ = f32[5,8,16,128]{3,2,1,0:T(8,128)S(1)} collective-permute-done((f32[5,8,16,128]{3,2,1,0:T(8,128)}, f32[5,8,16,128]{3,2,1,0:T(8,128)S(1)}, u32[]{:S(2)}, u32[]{:S(2)}) %collective-permute-start) | collective-permute-done | bytes 327712 | tf_op jit(solution)/shard_map/ppermute | solution.py:262
  31.8 0.5 collective-permute-start.4
  32.3 0.6 pad_add_fusion.where
  32.9 0.0 collective-permute-done.3.refs_4_
  32.9 0.0 collective-permute-done.6.refs_7_
  32.9 0.0 copy-start.4
  32.9 0.0 collective-permute-done.5.refs_6_
  32.9 0.0 copy-start.5
  32.9 0.6 collective-permute-done.4.refs_5_
  33.6 0.0 copy-done
  33.6 0.0 copy-done.1
  33.6 0.1 copy-done.3
  33.7 0.1 copy-done.4
  33.8 0.1 copy-done.5
  33.9 0.7 copy-done.6
  34.6 61.7 %shard_map.46 = f32[1,5,8,16,128]{4,3,2,1,0:T(8,128)} custom-call(s32[2]{0:T(128)} %pad_add_fusion.where, f32[5,8,16,128]{3,2,1,0:T(8,128)} %refs_0_.1, f32[5,8,16,128]{3,2,1,0:T(8,128)} %copy-done.2, f32[5,8,16,128]{3,2,1,0:T(8,128)} %copy-done.1, f32[5,8,16,128]{3,2,1,0:T(8,128)} %copy-done, f32[5,8,16,128]{3,2,1,0:T(8,128)} %copy-done.3, ...), custom_call_target="tpu_custom_call" | custom-call | tf_op jit(solution)/shard_map/pallas_call | solution.py:246
  (6 shorter events, 0.0 us)
Async XLA Ops:
  0.0 8.8 %collective-permute-start.2 = (f32[5,8,16,128]{3,2,1,0:T(8,128)}, f32[5,8,16,128]{3,2,1,0:T(8,128)S(1)}, u32[]{:S(2)}, u32[]{:S(2)}) collective-permute-start(f32[5,8,16,128]{3,2,1,0:T(8,128)} %refs_0_.1), channel_id=1, source_target_pairs={{6,0},{0,2},{2,4},{4,6},{7,1},{1,3},{3,5},{5,7},{14,8},{8,10},{10,... | collective-permute-start | bytes 983048 | tf_op jit(solution)/shard_map/ppermute | solution.py:262
  1.3 27.8 %collective-permute-start.1 = (f32[5,8,16,128]{3,2,1,0:T(8,128)}, f32[5,8,16,128]{3,2,1,0:T(8,128)S(1)}, u32[]{:S(2)}, u32[]{:S(2)}) collective-permute-start(f32[5,8,16,128]{3,2,1,0:T(8,128)} %refs_0_.1), channel_id=1, source_target_pairs={{4,0},{6,2},{0,4},{2,6},{5,1},{7,3},{1,5},{3,7},{12,8},{14,10},{8,... | collective-permute-start | bytes 983048 | tf_op jit(solution)/shard_map/ppermute | solution.py:262
  2.3 29.5 %collective-permute-start = (f32[5,8,16,128]{3,2,1,0:T(8,128)}, f32[5,8,16,128]{3,2,1,0:T(8,128)S(1)}, u32[]{:S(2)}, u32[]{:S(2)}) collective-permute-start(f32[5,8,16,128]{3,2,1,0:T(8,128)} %refs_0_.1), channel_id=1, source_target_pairs={{2,0},{4,2},{6,4},{0,6},{3,1},{5,3},{7,5},{1,7},{10,8},{12,10},{14... | collective-permute-start | bytes 983048 | tf_op jit(solution)/shard_map/ppermute | solution.py:262
  3.8 29.1 %collective-permute-start.3 = (f32[5,8,16,128]{3,2,1,0:T(8,128)}, f32[5,8,16,128]{3,2,1,0:T(8,128)S(1)}, u32[]{:S(2)}, u32[]{:S(2)}) collective-permute-start(f32[5,8,16,128]{3,2,1,0:T(8,128)} %refs_0_.1), channel_id=1, source_target_pairs={{0,1},{1,0},{2,3},{3,2},{4,5},{5,4},{6,7},{7,6},{8,9},{9,8},{10,11... | collective-permute-start | bytes 983048 | tf_op jit(solution)/shard_map/ppermute | solution.py:263
  8.8 24.8 %copy-start = (f32[5,8,16,128]{3,2,1,0:T(8,128)}, f32[5,8,16,128]{3,2,1,0:T(8,128)S(1)}, u32[]{:S(2)}) copy-start(f32[5,8,16,128]{3,2,1,0:T(8,128)S(1)} %collective-permute-done.2.refs_3_) | copy-start | bytes 983044
  8.8 24.1 %collective-permute-start.6 = (f32[5,8,16,128]{3,2,1,0:T(8,128)S(1)}, f32[5,8,16,128]{3,2,1,0:T(8,128)S(1)}, u32[]{:S(2)}, u32[]{:S(2)}) collective-permute-start(f32[5,8,16,128]{3,2,1,0:T(8,128)S(1)} %collective-permute-done.2.refs_3_), channel_id=1, source_target_pairs={{0,1},{1,0},{2,3},{3,2},{4,5},{5,4},{6,7},{7,6},{8,9},{9,8},{10,11... | collective-permute-start | bytes 983048 | tf_op jit(solution)/shard_map/ppermute | solution.py:263
  29.1 4.5 %copy-start.1 = (f32[5,8,16,128]{3,2,1,0:T(8,128)}, f32[5,8,16,128]{3,2,1,0:T(8,128)S(1)}, u32[]{:S(2)}) copy-start(f32[5,8,16,128]{3,2,1,0:T(8,128)S(1)} %collective-permute-done.1.refs_2_) | copy-start | bytes 983044
  29.1 3.9 %collective-permute-start.5 = (f32[5,8,16,128]{3,2,1,0:T(8,128)S(1)}, f32[5,8,16,128]{3,2,1,0:T(8,128)S(1)}, u32[]{:S(2)}, u32[]{:S(2)}) collective-permute-start(f32[5,8,16,128]{3,2,1,0:T(8,128)S(1)} %collective-permute-done.1.refs_2_), channel_id=1, source_target_pairs={{0,1},{1,0},{2,3},{3,2},{4,5},{5,4},{6,7},{7,6},{8,9},{9,8},{10,11... | collective-permute-start | bytes 983048 | tf_op jit(solution)/shard_map/ppermute | solution.py:263
  31.8 1.8 %copy-start.2 = (f32[5,8,16,128]{3,2,1,0:T(8,128)}, f32[5,8,16,128]{3,2,1,0:T(8,128)S(1)}, u32[]{:S(2)}) copy-start(f32[5,8,16,128]{3,2,1,0:T(8,128)S(1)} %collective-permute-done.refs_1_) | copy-start | bytes 983044
  31.8 1.8 %collective-permute-start.4 = (f32[5,8,16,128]{3,2,1,0:T(8,128)S(1)}, f32[5,8,16,128]{3,2,1,0:T(8,128)S(1)}, u32[]{:S(2)}, u32[]{:S(2)}) collective-permute-start(f32[5,8,16,128]{3,2,1,0:T(8,128)S(1)} %collective-permute-done.refs_1_), channel_id=1, source_target_pairs={{0,1},{1,0},{2,3},{3,2},{4,5},{5,4},{6,7},{7,6},{8,9},{9,8},{10,11... | collective-permute-start | bytes 983048 | tf_op jit(solution)/shard_map/ppermute | solution.py:263
  32.9 0.7 copy-start.3
  32.9 0.8 copy-start.4
  32.9 0.9 copy-start.5
  33.9 0.7 copy-start.6
where the time goes:
time: 96.5 us; the launch traced here: 96.3 us
  Pallas kernels  61.7 us (64%)
  starting transfers between devices  23.3 us (24%)
  waiting for transfers between devices  9.63 us (10%)
  local copies, waits for them, and re-layouts  1.05 us (1%)
    pallas_call x1, Pallas kernels, run_levels(): pl.pallas_call(functools.partial(levels_kernel, rows), out_shape=jax.Shap...  61.7 us
    ppermute x4, starting transfers between devices, gathered_body(): theirs = [lax.ppermute(piece, 'gy', [(0, 1), (1, 0)]) for piece in mine]  19.5 us
    ppermute x3, waiting for transfers between devices, gathered_body(): mine.append(lax.ppermute(state, 'gx', route))  9.02 us
    ppermute x3, starting transfers between devices, gathered_body(): mine.append(lax.ppermute(state, 'gx', route))  3.77 us
  transfers between devices with their start and end apart: 7, of which 4 were waited for; matrix products, arithmetic and copies ran while one was open for 1% of the time, Pallas kernels for 0%

commit v1 on v0

v1 whole, which is shorter than its diff:
```python
import functools

import jax
import jax.numpy as jnp
import ml_dtypes
import numpy as np
from jax import lax
from jax.experimental import pallas as pl
from jax.experimental.pallas import tpu as pltpu
from jax.sharding import PartitionSpec as P

STEPS = 3


DT = 0.1
GAMMA = 1.4
SHEAR_COEFFICIENT = 0.1
CONDUCTIVITY = 0.1
FIRST_COEF = (4.0 / 5.0, -1.0 / 5.0, 4.0 / 105.0, -1.0 / 280.0)
SECOND_CENTER = -205.0 / 72.0
SECOND_COEF = (8.0 / 5.0, -1.0 / 5.0, 8.0 / 315.0, -1.0 / 560.0)
REACH = 4
SCALE = 5040
FIRST_WHOLE = tuple(round(w * SCALE) for w in FIRST_COEF)
SECOND_WHOLE = tuple(round(w * SCALE) for w in SECOND_COEF)
VMEM_BUDGET = 56 * 1024 * 1024
FLUX_ROWS = 8
MIDDLE = 0.07


def circulants(extent):
    first = np.zeros((extent, extent), np.float32)
    second = np.zeros((extent, extent), np.float32)
    for place in range(extent):
        for k in range(1, REACH + 1):
            first[place, (place + k) % extent] -= FIRST_WHOLE[k - 1]
            first[place, (place - k) % extent] += FIRST_WHOLE[k - 1]
            second[place, (place + k) % extent] += SECOND_WHOLE[k - 1]
            second[place, (place - k) % extent] += SECOND_WHOLE[k - 1]
    return first, second


def split(value):
    high = value.astype(jnp.bfloat16)
    low = (value - high.astype(jnp.float32)).astype(jnp.bfloat16)
    return high, low


def levels_kernel(rows, n_near, n_far, where, *refs):
    near, far = refs[:n_near], refs[n_near : n_near + n_far]
    refs = refs[n_near + n_far :]
    wz_first, wz_second, wy, wxy, out = refs[:5]
    base, *held = refs[5:]
    fx, vis, part, G0, A1, A2, B1, A3, B2, C1, B3, C2, D1, C3, D2 = held
    fields, X, Y, Z = base.shape
    half = near[0].shape[2]
    level, side = where[0], where[1]
    own = (X - rows) // 2

    quarter = rows // 4

    def lay(value, core, ahead, e):
        at = pl.multiple_of(core * half, half)
        x = own + ahead * rows
        if e is None:
            base[:, x : x + rows, pl.ds(at, half), :] = value
        else:
            x = x + quarter * (level ^ e)
            x = jnp.where(x >= X, x - X, x)
            base[:, pl.ds(x, quarter), pl.ds(at, half), :] = value

    lay(near[0][...], side, 0, None)
    lay(far[0][...], 1 - side, 0, None)
    for ahead in range(1, X // rows):
        for e in range(4):
            lay(near[4 * ahead - 3 + e][...], side, ahead, e)
            lay(far[ahead][e], 1 - side, ahead, e)

    def pointwise(u):
        rho, m0, m1, m2, energy = u
        inverse = 1.0 / rho
        v0, v1, v2 = m0 * inverse, m1 * inverse, m2 * inverse
        m00, m11, m22 = m0 * v0, m1 * v1, m2 * v2
        m01, m02, m12 = m0 * v1, m0 * v2, m1 * v2
        twice = m00 + m11 + m22
        p = (GAMMA - 1.0) * energy - (0.5 * (GAMMA - 1.0)) * twice
        heat = energy + p
        warm = inverse * ((0.5 * SHEAR_COEFFICIENT) * twice + CONDUCTIVITY * p) - MIDDLE
        s = SHEAR_COEFFICIENT
        g = [s * v0, s * v1, s * v2, warm]
        along_x = [m0, m00 + p, m01, m02, heat * v0]
        along_y = [m1, m01, m11 + p, m12, heat * v1]
        along_z = [m2, m02, m12, m22 + p, heat * v2]
        return along_x, along_y, along_z, g

    def flux_rows(make, first, count, whole):
        batch = min(FLUX_ROWS, count)

        def step(i, carry):
            x = first + i * batch
            u = [make(f, x, batch).reshape(batch * Y, Z) for f in range(fields)]
            along_x, along_y, along_z, g = pointwise(u)
            for f in range(fields):
                fx[f, pl.ds(x + REACH, batch)] = along_x[f].reshape(batch, Y, Z)
            g = jnp.concatenate([v.astype(jnp.bfloat16) for v in g], axis=1)
            vis[pl.ds(pl.multiple_of((x + REACH) * Y, Y), batch * Y), :] = g
            if whole:
                zs = [split(v) for v in along_z]
                ys = [split(v) for v in along_y]
                flux = jnp.concatenate([jnp.concatenate(pair, axis=1) for pair in zs], axis=0)
                flux = jnp.dot(flux, wz_first[...], preferred_element_type=jnp.float32)
                soft = jnp.concatenate([g[:, : 2 * Z], g[:, 2 * Z :]], axis=0)
                soft = jnp.dot(soft, wz_second[...], preferred_element_type=jnp.float32)
                group = wy.shape[0] // Y
                for r in range(0, batch, group):
                    columns = []
                    for f in range(fields):
                        cuts = [slice((r + q) * Y, (r + q + 1) * Y) for q in range(group)]
                        columns.append(jnp.concatenate([v[cut] for cut in cuts for v in ys[f]], axis=0))
                    deep = jnp.dot(wy[...], jnp.concatenate(columns, axis=1), preferred_element_type=jnp.float32)
                    for f in range(fields):
                        at = f * batch * Y + r * Y
                        total = deep[:, f * Z : (f + 1) * Z] + flux[at : at + group * Y]
                        if f:
                            at = ((f - 1) // 2) * batch * Y + r * Y
                            lane = ((f - 1) % 2) * Z
                            total = total + soft[at : at + group * Y, lane : lane + Z]
                        part[f, pl.ds(x + r, group)] = total.reshape(group, Y, Z)
            return carry

        lax.fori_loop(0, count // batch, step, 0)

    def stencil_rows(target, shift, first, count):
        block = wxy.shape[0] // Y

        def soften(x):
            g = [vis[x * Y : (x + block + 2 * REACH) * Y, 2 * p * Z : 2 * (p + 1) * Z] for p in range(2)]
            return [jnp.dot(wxy[...], v, preferred_element_type=jnp.float32).reshape(block, Y, 2 * Z) for v in g]

        def end(x, soft):
            for f in range(fields):
                for y in range(0, Y, 8):
                    flux = fx[f, x : x + block + 2 * REACH, y : y + 8, :]
                    total = part[f, x : x + block, y : y + 8, :]
                    if f:
                        pair, place = divmod(f - 1, 2)
                        total = total + soft[pair][:, y : y + 8, place * Z : (place + 1) * Z]
                    for k in range(1, REACH + 1):
                        ahead = slice(REACH + k, REACH + k + block)
                        behind = slice(REACH - k, REACH - k + block)
                        total = total + float(FIRST_WHOLE[k - 1]) * (flux[behind] - flux[ahead])
                    target[f, x - shift : x - shift + block, y : y + 8, :] = (DT / SCALE) * total

        places = range(first, first + count, block)
        soft = soften(places[0])
        for x in places:
            following = soften(x + block) if x + block < first + count else None
            end(x, soft)
            soft = following

    def tendency(target, make, reach):
        first, count = own - reach, rows + 2 * reach
        if count >= X:
            first, count = 0, X
            flux_rows(make, 0, X, True)
            edge = REACH * Y
            fx[:, :REACH] = fx[:, X : X + REACH]
            fx[:, X + REACH :] = fx[:, REACH : 2 * REACH]
            vis[:edge] = vis[X * Y : X * Y + edge]
            vis[X * Y + edge :] = vis[edge : 2 * edge]
        else:
            flux_rows(make, first, count, True)
            flux_rows(make, first - REACH, REACH, False)
            flux_rows(make, first + count, REACH, False)
        stencil_rows(target, first, first, count)

    def rows_of(ref, f, x, n):
        return ref[f, pl.ds(x - (X - ref.shape[1]) // 2, n)]

    half_step, five, sixth, twelfth = 0.5, 5.0 / 12.0, 1.0 / 6.0, 1.0 / 12.0

    def mix(*terms):
        def make(f, x, n):
            total = None
            for weight, *held in terms:
                value = rows_of(held[0], f, x, n)
                for ref in held[1:]:
                    value = value + rows_of(ref, f, x, n)
                value = value if weight == 1 else weight * value
                total = value if total is None else total + value
            return total

        return make

    def second(g, low, mid, high):
        return mix((1, base, mid), (five, g, high), (sixth, low))

    u03 = ((1, base, G0, A1, A2),)
    u13 = ((1, base, B1, B2), (five, G0, A3), (twelfth, A1, A2))
    u23 = ((1, base, C1, C2), (five, G0, B3), (twelfth, B1, B2))
    u33 = ((1, base, D1, D2), (five, G0, C3), (twelfth, C1, C2))

    tendency(G0, mix((1, base)), 5 * REACH)
    tendency(A1, mix((1, base, G0)), 4 * REACH)
    tendency(A2, mix((1, base, G0, A1)), 3 * REACH)
    tendency(B1, mix((1, base), (half_step, G0, A1)), 3 * REACH)
    tendency(A3, mix(*u03), 2 * REACH)
    tendency(B2, second(G0, A1, B1, A2), 2 * REACH)
    tendency(C1, mix((1, base), (half_step, G0, B1)), 2 * REACH)
    tendency(B3, mix(*u13), REACH)
    tendency(C2, second(G0, B1, C1, B2), REACH)
    tendency(D1, mix((1, base), (half_step, G0, C1)), REACH)
    tendency(C3, mix(*u23), 0)
    tendency(D2, second(G0, C1, D1, C2), 0)

    at = pl.multiple_of(side * half, half)
    for p, terms in enumerate((u03, u13, u23, u33)):

        @pl.when(level == p)
        def _():
            for f in range(fields):
                total = None
                for weight, *held in terms:
                    value = None
                    for ref in held:
                        start = own - (X - ref.shape[1]) // 2
                        here = ref[f, start : start + rows, pl.ds(at, half), :]
                        value = here if value is None else value + here
                    value = value if weight == 1 else weight * value
                    total = value if total is None else total + value
                out[0, f] = total


def run_levels(where, near, far, gx):
    fields, rows, half, Z = near[0].shape
    X, Y = rows * gx, 2 * half
    bf16 = ml_dtypes.bfloat16
    first_z, second_z = circulants(Z)
    first_y, second_y = circulants(Y)
    centre = round(3 * SECOND_CENTER * SCALE)
    coarse = int(np.float32(bf16(centre)))
    second_z = second_z + (centre - coarse) * np.eye(Z, dtype=np.float32)
    second_y = second_y + coarse * np.eye(Y, dtype=np.float32)
    wz_first = np.concatenate([first_z.T, first_z.T], axis=0).astype(bf16)
    wz_second = np.kron(np.eye(2, dtype=np.float32), second_z.T).astype(bf16)
    group = max(1, 128 // Y)
    wy = np.kron(np.eye(group, dtype=np.float32), np.concatenate([first_y, first_y], axis=1)).astype(bf16)
    block = rows
    wxy = np.zeros((block, Y, block + 2 * REACH, Y), np.float32)
    for x in range(block):
        wxy[x, :, x + REACH, :] = second_y
        for k in range(1, REACH + 1):
            wxy[x, :, x + REACH + k, :] = SECOND_WHOLE[k - 1] * np.eye(Y, dtype=np.float32)
            wxy[x, :, x + REACH - k, :] = SECOND_WHOLE[k - 1] * np.eye(Y, dtype=np.float32)
    wxy = wxy.reshape(block * Y, (block + 2 * REACH) * Y).astype(bf16)

    def hold(n):
        return pltpu.VMEM((fields, n, Y, Z), jnp.float32)

    soft = pltpu.VMEM(((X + 2 * REACH) * Y, (fields - 1) * Z), jnp.bfloat16)
    scratch = [hold(X), hold(X + 2 * REACH), soft, hold(X)]
    for reach in (5, 4, 3, 3, 2, 2, 2, 1, 1, 1, 0, 0):
        scratch.append(hold(min(X, rows + 2 * reach * REACH)))
    vmem = pl.BlockSpec(memory_space=pltpu.VMEM)
    return pl.pallas_call(
        functools.partial(levels_kernel, rows, len(near), len(far)),
        out_shape=jax.ShapeDtypeStruct((1, fields, rows, half, Z), jnp.float32),
        in_specs=[pl.BlockSpec(memory_space=pltpu.SMEM)] + [vmem] * (len(near) + len(far) + 4),
        out_specs=vmem,
        scratch_shapes=scratch,
        compiler_params=pltpu.CompilerParams(vmem_limit_bytes=VMEM_BUDGET),
    )(where, *near, *far, wz_first, wz_second, wy, wxy)


def gathered_body(state):
    gx, levels = lax.axis_size("gx"), lax.axis_size("level")
    level = lax.axis_index("level")
    where = jnp.stack([level, lax.axis_index("gy")]).astype(jnp.int32)
    swap = [(0, 1), (1, 0)]
    quarter = state.shape[1] // levels
    mine = lax.dynamic_slice_in_dim(state, level * quarter, quarter, axis=1)
    near, far = [state], [lax.ppermute(state, "gy", swap)]
    for ahead in range(1, gx):
        route = [((i + ahead) % gx, i) for i in range(gx)]
        first = lax.ppermute(mine, "gx", route)
        parts = [first]
        for e in range(1, levels):
            parts.append(lax.ppermute(first, "level", [(i, i ^ e) for i in range(levels)]))
        near += parts
        far.append(lax.ppermute(jnp.stack(parts), "gy", swap))
    return run_levels(where, near, far, gx)


def with_halo(block, sides, width):
    for axis, dim in sides:
        count = lax.axis_size(axis)
        forward = [(i, i + 1) for i in range(count - 1)]
        forward.append((count - 1, 0))
        backward = [(target, source) for source, target in forward]
        low = lax.ppermute(
            lax.slice_in_dim(block, block.shape[dim] - width, None, axis=dim), axis, forward
        )
        high = lax.ppermute(lax.slice_in_dim(block, 0, width, axis=dim), axis, backward)
        block = jnp.concatenate([low, block, high], axis=dim)
    return block


def shifted_2(block, axis, distance):
    devices = range(lax.axis_size(axis))
    route = [(i - distance, i) for i in devices if i - distance in devices]
    return lax.ppermute(block, axis, route)


def shifted(quantity, direction, offset):
    extent = quantity.shape[-3:]
    picks = [slice(4, extent[0] - 4), slice(4, extent[1] - 4), slice(4, extent[2] - 4)]
    picks[direction] = slice(4 + offset, extent[direction] - 4 + offset)
    leading = (slice(None),) * (quantity.ndim - 3)
    return quantity[leading + tuple(picks)]


def first_derivative(quantity, direction):
    total = 0.0
    for position, weight in enumerate(FIRST_COEF):
        total = total + weight * (
            shifted(quantity, direction, position + 1) - shifted(quantity, direction, -position - 1)
        )
    return total


def second_derivative_sum(quantity):
    total = 0.0
    for direction in range(3):
        total = total + SECOND_CENTER * shifted(quantity, direction, 0)
        for position, weight in enumerate(SECOND_COEF):
            total = total + weight * (
                shifted(quantity, direction, position + 1)
                + shifted(quantity, direction, -position - 1)
            )
    return total


def tendency(padded):
    specific_volume_inverse = padded[0]
    momentum = padded[1:4]
    energy = padded[4]
    velocity = momentum / specific_volume_inverse
    kinetic_energy_share = 0.5 * jnp.sum(velocity * velocity, axis=0)
    normal_stress_scalar = (GAMMA - 1.0) * (energy - specific_volume_inverse * kinetic_energy_share)
    absolute_kelvin_value = normal_stress_scalar / specific_volume_inverse
    divergence = 0.0
    for direction in range(3):
        along = velocity[direction]
        rows = [
            momentum[component] * along + (normal_stress_scalar if component == direction else 0.0)
            for component in range(3)
        ]
        flux = jnp.stack([momentum[direction]] + rows + [(energy + normal_stress_scalar) * along])
        divergence = divergence + first_derivative(flux, direction)
    viscous = SHEAR_COEFFICIENT * second_derivative_sum(velocity)
    conduction_contribution = SHEAR_COEFFICIENT * second_derivative_sum(
        kinetic_energy_share
    ) + CONDUCTIVITY * second_derivative_sum(absolute_kelvin_value)
    return jnp.concatenate(
        [
            -divergence[0:1],
            viscous - divergence[1:4],
            (conduction_contribution - divergence[4])[None],
        ],
        axis=0,
    )


def wrap_depth(field):
    return jnp.concatenate([field[:, :, :, -4:], field, field[:, :, :, :4]], axis=3)


def padded_faces(field):
    return wrap_depth(with_halo(field, (("gx", 1), ("gy", 2)), 4))


def sections_body(state):
    levels = lax.axis_size("level")
    rank = lax.axis_index("level")
    current = state
    before = jnp.zeros_like(state)
    middle = jnp.zeros_like(state)
    for section in range(STEPS + levels - 1):
        node = section - rank
        forcing = tendency(padded_faces(current))
        newest = shifted_2(forcing, "level", 1)
        quad_term = jnp.where(
            node == 0, 0.5 * (middle + newest), (8.0 * middle + 5.0 * newest - before) / 12.0
        )
        moved = current + DT * (forcing - middle + quad_term)
        active = jnp.logical_and(node >= 0, node < STEPS)
        current = jnp.where(active, moved, current)
        before = middle
        middle = newest
    return current[None]


def body(state):
    fields, rows, half, Z = state.shape
    gx, gy, levels = lax.axis_size("gx"), lax.axis_size("gy"), lax.axis_size("level")
    X, Y = rows * gx, half * gy
    need = 4 * fields * Y * Z * 15 * X
    simple = gy == 2 and levels == 4 and Z == 128 and Y % 32 == 0 and rows == 2 * REACH and rows % levels == 0 and half % 16 == 0
    if simple and gx % 2 == 0 and X <= rows + 6 * REACH and need <= VMEM_BUDGET:
        return gathered_body(state)
    return sections_body(state)


def solution(mesh):
    return jax.shard_map(
        body,
        mesh=mesh,
        in_specs=(P(None, "gx", "gy", None),),
        out_specs=P("level", None, "gx", "gy", None),
        check_vma=False,
    )
```

time: 96.5 us -> 73.2 us (0.76)
  the two profiles are of different devices: /device:TPU:15 before, /device:TPU:19 now
where the time goes in v1:
time: 73.2 us; the launch traced here: 73 us
  Pallas kernels  42.4 us (58%)
  starting transfers between devices  21.9 us (30%)
  waiting for transfers between devices  5.35 us (7%)
  local copies, waits for them, and re-layouts  2.58 us (4%)
    pallas_call x1, Pallas kernels, run_levels(): pl.pallas_call(functools.partial(levels_kernel, rows, len(near), len(far)...  42.4 us
    ppermute x9, starting transfers between devices, gathered_body(): lax.ppermute(first, 'level', [(i, i ^ e) for i in range(levels)])  8.1 us
    ppermute x1, starting transfers between devices, gathered_body(): near, far = ([state], [lax.ppermute(state, 'gy', swap)])  6.5 us
    ppermute x3, starting transfers between devices, gathered_body(): far.append(lax.ppermute(jnp.stack(parts), 'gy', swap))  4.7 us
    ppermute x9, waiting for transfers between devices, gathered_body(): lax.ppermute(first, 'level', [(i, i ^ e) for i in range(levels)])  3.5 us
    ppermute x3, starting transfers between devices, gathered_body(): first = lax.ppermute(mine, 'gx', route)  2.55 us
    unnamed x32, local copies, waits for them, and re-layouts  1.68 us
  transfers between devices with their start and end apart: 16, of which 6 were waited for; matrix products, arithmetic and copies ran while one was open for 1% of the time, Pallas kernels for 0%

profile of v1, /device:TPU:19, one launch (start us, length us, event | category | flops | bytes accessed | tf_op | source)
XLA Modules:
  0.0 73.0 jit_solution(11060623567125426776)
XLA Ops:
  0.0 0.9 %constant_dynamic-slice_fusion = f32[5,2,16,128]{3,2,1,0:T(8,128)S(1)} fusion(f32[5,8,16,128]{3,2,1,0:T(8,128)} %refs_0_.1, s32[]{:T(128)S(6)} %select_n.3), kind=kLoop, calls=%fused_computation.4 | loop fusion | bytes 163844 | tf_op jit(solution)/shard_map/dynamic_slice | solution.py:281
  0.9 1.3 %collective-permute-start.8 = (f32[5,2,16,128]{3,2,1,0:T(8,128)S(1)}, f32[5,2,16,128]{3,2,1,0:T(8,128)S(1)}, u32[]{:S(2)}, u32[]{:S(2)}) collective-permute-start(f32[5,2,16,128]{3,2,1,0:T(8,128)S(1)} %constant_dynamic-slice_fusion), channel_id=1, source_target_pairs={{6,0},{0,2},{2,4},{4,6},{7,1},{1,3},{3,5},{5,7},{14,8},{8,10},{10,... | collective-permute-start | bytes 245768 | tf_op jit(solution)/shard_map/ppermute | solution.py:285
  2.2 1.2 %collective-permute-start = (f32[5,2,16,128]{3,2,1,0:T(8,128)S(1)}, f32[5,2,16,128]{3,2,1,0:T(8,128)S(1)}, u32[]{:S(2)}, u32[]{:S(2)}) collective-permute-start(f32[5,2,16,128]{3,2,1,0:T(8,128)S(1)} %constant_dynamic-slice_fusion), channel_id=1, source_target_pairs={{2,0},{4,2},{6,4},{0,6},{3,1},{5,3},{7,5},{1,7},{10,8},{12,10},{14... | collective-permute-start | bytes 245768 | tf_op jit(solution)/shard_map/ppermute | solution.py:285
  3.4 0.7 %collective-permute-done.8.refs_9_ = f32[5,2,16,128]{3,2,1,0:T(8,128)S(1)} collective-permute-done((f32[5,2,16,128]{3,2,1,0:T(8,128)S(1)}, f32[5,2,16,128]{3,2,1,0:T(8,128)S(1)}, u32[]{:S(2)}, u32[]{:S(2)}) %collective-permute-start.8) | collective-permute-done | bytes 81952 | tf_op jit(solution)/shard_map/ppermute | solution.py:285
  4.2 1.2 %collective-permute-start.11 = (f32[5,2,16,128]{3,2,1,0:T(8,128)S(1)}, f32[5,2,16,128]{3,2,1,0:T(8,128)S(1)}, u32[]{:S(2)}, u32[]{:S(2)}) collective-permute-start(f32[5,2,16,128]{3,2,1,0:T(8,128)S(1)} %collective-permute-done.8.refs_9_), channel_id=1, source_target_pairs={{0,24},{8,16},{16,8},{24,0},{1,25},{9,17},{17,9},{25,1},{2,26},{10... | collective-permute-start | bytes 245768 | tf_op jit(solution)/shard_map/ppermute | solution.py:288
  5.6 1.2 %collective-permute-start.9 = (f32[5,2,16,128]{3,2,1,0:T(8,128)S(1)}, f32[5,2,16,128]{3,2,1,0:T(8,128)S(1)}, u32[]{:S(2)}, u32[]{:S(2)}) collective-permute-start(f32[5,2,16,128]{3,2,1,0:T(8,128)S(1)} %collective-permute-done.8.refs_9_), channel_id=1, source_target_pairs={{0,8},{8,0},{16,24},{24,16},{1,9},{9,1},{17,25},{25,17},{2,10},{10... | collective-permute-start | bytes 245768 | tf_op jit(solution)/shard_map/ppermute | solution.py:288
  6.8 0.5 collective-permute-done.4.refs_5_
  7.3 6.5 %collective-permute-start.12 = (f32[5,8,16,128]{3,2,1,0:T(8,128)}, f32[5,8,16,128]{3,2,1,0:T(8,128)S(1)}, u32[]{:S(2)}, u32[]{:S(2)}) collective-permute-start(f32[5,8,16,128]{3,2,1,0:T(8,128)} %refs_0_.1), channel_id=1, source_target_pairs={{0,1},{1,0},{2,3},{3,2},{4,5},{5,4},{6,7},{7,6},{8,9},{9,8},{10,11... | collective-permute-start | bytes 983048 | tf_op jit(solution)/shard_map/ppermute | solution.py:282
  13.9 1.2 %collective-permute-start.7 = (f32[5,2,16,128]{3,2,1,0:T(8,128)S(1)}, f32[5,2,16,128]{3,2,1,0:T(8,128)S(1)}, u32[]{:S(2)}, u32[]{:S(2)}) collective-permute-start(f32[5,2,16,128]{3,2,1,0:T(8,128)S(1)} %collective-permute-done.4.refs_5_), channel_id=1, source_target_pairs={{0,24},{8,16},{16,8},{24,0},{1,25},{9,17},{17,9},{25,1},{2,26},{10... | collective-permute-start | bytes 245768 | tf_op jit(solution)/shard_map/ppermute | solution.py:288
  15.3 1.2 %collective-permute-start.5 = (f32[5,2,16,128]{3,2,1,0:T(8,128)S(1)}, f32[5,2,16,128]{3,2,1,0:T(8,128)S(1)}, u32[]{:S(2)}, u32[]{:S(2)}) collective-permute-start(f32[5,2,16,128]{3,2,1,0:T(8,128)S(1)} %collective-permute-done.4.refs_5_), channel_id=1, source_target_pairs={{0,8},{8,0},{16,24},{24,16},{1,9},{9,1},{17,25},{25,17},{2,10},{10... | collective-permute-start | bytes 245768 | tf_op jit(solution)/shard_map/ppermute | solution.py:288
  16.5 1.2 %collective-permute-start.3 = (f32[5,2,16,128]{3,2,1,0:T(8,128)S(1)}, f32[5,2,16,128]{3,2,1,0:T(8,128)S(1)}, u32[]{:S(2)}, u32[]{:S(2)}) collective-permute-start(f32[5,2,16,128]{3,2,1,0:T(8,128)S(1)} %collective-permute-done.refs_1_), channel_id=1, source_target_pairs={{0,24},{8,16},{16,8},{24,0},{1,25},{9,17},{17,9},{25,1},{2,26},{10... | collective-permute-start | bytes 245768 | tf_op jit(solution)/shard_map/ppermute | solution.py:288
  17.8 1.0 %collective-permute-done.7.refs_8_ = f32[5,2,16,128]{3,2,1,0:T(8,128)S(1)} collective-permute-done((f32[5,2,16,128]{3,2,1,0:T(8,128)S(1)}, f32[5,2,16,128]{3,2,1,0:T(8,128)S(1)}, u32[]{:S(2)}, u32[]{:S(2)}) %collective-permute-start.7) | collective-permute-done | bytes 81952 | tf_op jit(solution)/shard_map/ppermute | solution.py:288
  18.8 1.3 %collective-permute-start.2 = (f32[5,2,16,128]{3,2,1,0:T(8,128)S(1)}, f32[5,2,16,128]{3,2,1,0:T(8,128)S(1)}, u32[]{:S(2)}, u32[]{:S(2)}) collective-permute-start(f32[5,2,16,128]{3,2,1,0:T(8,128)S(1)} %collective-permute-done.refs_1_), channel_id=1, source_target_pairs={{0,16},{8,24},{16,0},{24,8},{1,17},{9,25},{17,1},{25,9},{2,18},{10... | collective-permute-start | bytes 245768 | tf_op jit(solution)/shard_map/ppermute | solution.py:288
  20.1 1.7 %collective-permute-done.6.refs_7_ = f32[5,2,16,128]{3,2,1,0:T(8,128)S(1)} collective-permute-done((f32[5,2,16,128]{3,2,1,0:T(8,128)S(1)}, f32[5,2,16,128]{3,2,1,0:T(8,128)S(1)}, u32[]{:S(2)}, u32[]{:S(2)}) %collective-permute-start.6) | collective-permute-done | bytes 81952 | tf_op jit(solution)/shard_map/ppermute | solution.py:288
  21.8 0.3 collective-permute-start.1
  22.1 1.5 %collective-permute-start.15 = (f32[4,5,2,16,128]{4,3,2,1,0:T(8,128)S(1)}, f32[4,5,2,16,128]{4,3,2,1,0:T(8,128)S(1)}, u32[]{:S(2)}, u32[]{:S(2)}) collective-permute-start(f32[4,5,2,16,128]{4,3,2,1,0:T(8,128)S(1)} %pad_maximum_fusion.2), channel_id=1, source_target_pairs={{0,1},{1,0},{2,3},{3,2},{4,5},{5,4},{6,7},{7,6},{8,9},{9,8},{10,11... | collective-permute-start | bytes 983048 | tf_op jit(solution)/shard_map/ppermute | solution.py:290
  23.7 0.6 collective-permute-start.14
  24.2 0.8 %collective-permute-done.1.refs_2_ = f32[5,2,16,128]{3,2,1,0:T(8,128)S(1)} collective-permute-done((f32[5,2,16,128]{3,2,1,0:T(8,128)S(1)}, f32[5,2,16,128]{3,2,1,0:T(8,128)S(1)}, u32[]{:S(2)}, u32[]{:S(2)}) %collective-permute-start.1) | collective-permute-done | bytes 81952 | tf_op jit(solution)/shard_map/ppermute | solution.py:288
  25.1 0.6 copy-done.11
  25.7 2.6 %collective-permute-start.13 = (f32[4,5,2,16,128]{4,3,2,1,0:T(8,128)S(1)}, f32[4,5,2,16,128]{4,3,2,1,0:T(8,128)S(1)}, u32[]{:S(2)}, u32[]{:S(2)}) collective-permute-start(f32[4,5,2,16,128]{4,3,2,1,0:T(8,128)S(1)} %pad_maximum_fusion), channel_id=1, source_target_pairs={{0,1},{1,0},{2,3},{3,2},{4,5},{5,4},{6,7},{7,6},{8,9},{9,8},{10,11... | collective-permute-start | bytes 983048 | tf_op jit(solution)/shard_map/ppermute | solution.py:290
  28.3 0.6 pad_add_fusion.where
  29.0 0.6 collective-permute-done.13.refs_14_
  29.9 0.7 copy-done.15
  30.6 42.4 %shard_map.55 = f32[1,5,8,16,128]{4,3,2,1,0:T(8,128)} custom-call(s32[2]{0:T(128)} %pad_add_fusion.where, f32[5,8,16,128]{3,2,1,0:T(8,128)} %refs_0_.1, f32[5,2,16,128]{3,2,1,0:T(8,128)} %copy-done.2, f32[5,2,16,128]{3,2,1,0:T(8,128)} %copy-done.11, f32[5,2,16,128]{3,2,1,0:T(8,128)} %copy-done.10, f32[5,2,16,128]{3,2,1,0:T(8,128)} %copy-done.9, ...), custom_call_target="tpu_custom_call" | custom-call | tf_op jit(solution)/shard_map/pallas_call | solution.py:265
  (46 shorter events, 1.0 us)
Async XLA Ops:
  0.9 3.3 %collective-permute-start.8 = (f32[5,2,16,128]{3,2,1,0:T(8,128)S(1)}, f32[5,2,16,128]{3,2,1,0:T(8,128)S(1)}, u32[]{:S(2)}, u32[]{:S(2)}) collective-permute-start(f32[5,2,16,128]{3,2,1,0:T(8,128)S(1)} %constant_dynamic-slice_fusion), channel_id=1, source_target_pairs={{6,0},{0,2},{2,4},{4,6},{7,1},{1,3},{3,5},{5,7},{14,8},{8,10},{10,... | collective-permute-start | bytes 245768 | tf_op jit(solution)/shard_map/ppermute | solution.py:285
  2.2 5.2 %collective-permute-start.4 = (f32[5,2,16,128]{3,2,1,0:T(8,128)S(1)}, f32[5,2,16,128]{3,2,1,0:T(8,128)S(1)}, u32[]{:S(2)}, u32[]{:S(2)}) collective-permute-start(f32[5,2,16,128]{3,2,1,0:T(8,128)S(1)} %constant_dynamic-slice_fusion), channel_id=1, source_target_pairs={{4,0},{6,2},{0,4},{2,6},{5,1},{7,3},{1,5},{3,7},{12,8},{14,10},{8,... | collective-permute-start | bytes 245768 | tf_op jit(solution)/shard_map/ppermute | solution.py:285
  2.2 11.6 %collective-permute-start = (f32[5,2,16,128]{3,2,1,0:T(8,128)S(1)}, f32[5,2,16,128]{3,2,1,0:T(8,128)S(1)}, u32[]{:S(2)}, u32[]{:S(2)}) collective-permute-start(f32[5,2,16,128]{3,2,1,0:T(8,128)S(1)} %constant_dynamic-slice_fusion), channel_id=1, source_target_pairs={{2,0},{4,2},{6,4},{0,6},{3,1},{5,3},{7,5},{1,7},{10,8},{12,10},{14... | collective-permute-start | bytes 245768 | tf_op jit(solution)/shard_map/ppermute | solution.py:285
  4.2 13.6 %copy-start = (f32[5,2,16,128]{3,2,1,0:T(8,128)}, f32[5,2,16,128]{3,2,1,0:T(8,128)S(1)}, u32[]{:S(2)}) copy-start(f32[5,2,16,128]{3,2,1,0:T(8,128)S(1)} %collective-permute-done.8.refs_9_) | copy-start | bytes 245764
  4.2 10.9 %collective-permute-start.11 = (f32[5,2,16,128]{3,2,1,0:T(8,128)S(1)}, f32[5,2,16,128]{3,2,1,0:T(8,128)S(1)}, u32[]{:S(2)}, u32[]{:S(2)}) collective-permute-start(f32[5,2,16,128]{3,2,1,0:T(8,128)S(1)} %collective-permute-done.8.refs_9_), channel_id=1, source_target_pairs={{0,24},{8,16},{16,8},{24,0},{1,25},{9,17},{17,9},{25,1},{2,26},{10... | collective-permute-start | bytes 245768 | tf_op jit(solution)/shard_map/ppermute | solution.py:288
  5.4 9.9 %collective-permute-start.10 = (f32[5,2,16,128]{3,2,1,0:T(8,128)S(1)}, f32[5,2,16,128]{3,2,1,0:T(8,128)S(1)}, u32[]{:S(2)}, u32[]{:S(2)}) collective-permute-start(f32[5,2,16,128]{3,2,1,0:T(8,128)S(1)} %collective-permute-done.8.refs_9_), channel_id=1, source_target_pairs={{0,16},{8,24},{16,0},{24,8},{1,17},{9,25},{17,1},{25,9},{2,18},{10... | collective-permute-start | bytes 245768 | tf_op jit(solution)/shard_map/ppermute | solution.py:288
  5.6 10.9 %collective-permute-start.9 = (f32[5,2,16,128]{3,2,1,0:T(8,128)S(1)}, f32[5,2,16,128]{3,2,1,0:T(8,128)S(1)}, u32[]{:S(2)}, u32[]{:S(2)}) collective-permute-start(f32[5,2,16,128]{3,2,1,0:T(8,128)S(1)} %collective-permute-done.8.refs_9_), channel_id=1, source_target_pairs={{0,8},{8,0},{16,24},{24,16},{1,9},{9,1},{17,25},{25,17},{2,10},{10... | collective-permute-start | bytes 245768 | tf_op jit(solution)/shard_map/ppermute | solution.py:288
  7.3 16.3 %copy-start.1 = (f32[5,2,16,128]{3,2,1,0:T(8,128)}, f32[5,2,16,128]{3,2,1,0:T(8,128)S(1)}, u32[]{:S(2)}) copy-start(f32[5,2,16,128]{3,2,1,0:T(8,128)S(1)} %collective-permute-done.4.refs_5_) | copy-start | bytes 245764
  7.3 21.6 %collective-permute-start.12 = (f32[5,8,16,128]{3,2,1,0:T(8,128)}, f32[5,8,16,128]{3,2,1,0:T(8,128)S(1)}, u32[]{:S(2)}, u32[]{:S(2)}) collective-permute-start(f32[5,8,16,128]{3,2,1,0:T(8,128)} %refs_0_.1), channel_id=1, source_target_pairs={{0,1},{1,0},{2,3},{3,2},{4,5},{5,4},{6,7},{7,6},{8,9},{9,8},{10,11... | collective-permute-start | bytes 983048 | tf_op jit(solution)/shard_map/ppermute | solution.py:282
  13.8 11.2 %copy-start.2 = (f32[5,2,16,128]{3,2,1,0:T(8,128)}, f32[5,2,16,128]{3,2,1,0:T(8,128)S(1)}, u32[]{:S(2)}) copy-start(f32[5,2,16,128]{3,2,1,0:T(8,128)S(1)} %collective-permute-done.refs_1_) | copy-start | bytes 245764
  13.9 4.9 %collective-permute-start.7 = (f32[5,2,16,128]{3,2,1,0:T(8,128)S(1)}, f32[5,2,16,128]{3,2,1,0:T(8,128)S(1)}, u32[]{:S(2)}, u32[]{:S(2)}) collective-permute-start(f32[5,2,16,128]{3,2,1,0:T(8,128)S(1)} %collective-permute-done.4.refs_5_), channel_id=1, source_target_pairs={{0,24},{8,16},{16,8},{24,0},{1,25},{9,17},{17,9},{25,1},{2,26},{10... | collective-permute-start | bytes 245768 | tf_op jit(solution)/shard_map/ppermute | solution.py:288
  15.1 2.7 %copy-start.3 = (f32[5,2,16,128]{3,2,1,0:T(8,128)}, f32[5,2,16,128]{3,2,1,0:T(8,128)S(1)}, u32[]{:S(2)}) copy-start(f32[5,2,16,128]{3,2,1,0:T(8,128)S(1)} %collective-permute-done.11.refs_12_) | copy-start | bytes 245764
  15.1 6.7 %collective-permute-start.6 = (f32[5,2,16,128]{3,2,1,0:T(8,128)S(1)}, f32[5,2,16,128]{3,2,1,0:T(8,128)S(1)}, u32[]{:S(2)}, u32[]{:S(2)}) collective-permute-start(f32[5,2,16,128]{3,2,1,0:T(8,128)S(1)} %collective-permute-done.4.refs_5_), channel_id=1, source_target_pairs={{0,16},{8,24},{16,0},{24,8},{1,17},{9,25},{17,1},{25,9},{2,18},{10... | collective-permute-start | bytes 245768 | tf_op jit(solution)/shard_map/ppermute | solution.py:288
  15.3 2.5 %copy-start.4 = (f32[5,2,16,128]{3,2,1,0:T(8,128)}, f32[5,2,16,128]{3,2,1,0:T(8,128)S(1)}, u32[]{:S(2)}) copy-start(f32[5,2,16,128]{3,2,1,0:T(8,128)S(1)} %collective-permute-done.10.refs_11_) | copy-start | bytes 245764
  15.3 6.7 %collective-permute-start.5 = (f32[5,2,16,128]{3,2,1,0:T(8,128)S(1)}, f32[5,2,16,128]{3,2,1,0:T(8,128)S(1)}, u32[]{:S(2)}, u32[]{:S(2)}) collective-permute-start(f32[5,2,16,128]{3,2,1,0:T(8,128)S(1)} %collective-permute-done.4.refs_5_), channel_id=1, source_target_pairs={{0,8},{8,0},{16,24},{24,16},{1,9},{9,1},{17,25},{25,17},{2,10},{10... | collective-permute-start | bytes 245768 | tf_op jit(solution)/shard_map/ppermute | solution.py:288
  16.5 7.1 %collective-permute-start.3 = (f32[5,2,16,128]{3,2,1,0:T(8,128)S(1)}, f32[5,2,16,128]{3,2,1,0:T(8,128)S(1)}, u32[]{:S(2)}, u32[]{:S(2)}) collective-permute-start(f32[5,2,16,128]{3,2,1,0:T(8,128)S(1)} %collective-permute-done.refs_1_), channel_id=1, source_target_pairs={{0,24},{8,16},{16,8},{24,0},{1,25},{9,17},{17,9},{25,1},{2,26},{10... | collective-permute-start | bytes 245768 | tf_op jit(solution)/shard_map/ppermute | solution.py:288
  18.8 4.9 %copy-start.6 = (f32[5,2,16,128]{3,2,1,0:T(8,128)}, f32[5,2,16,128]{3,2,1,0:T(8,128)S(1)}, u32[]{:S(2)}) copy-start(f32[5,2,16,128]{3,2,1,0:T(8,128)S(1)} %collective-permute-done.7.refs_8_) | copy-start | bytes 245764
  18.8 5.5 %collective-permute-start.2 = (f32[5,2,16,128]{3,2,1,0:T(8,128)S(1)}, f32[5,2,16,128]{3,2,1,0:T(8,128)S(1)}, u32[]{:S(2)}, u32[]{:S(2)}) collective-permute-start(f32[5,2,16,128]{3,2,1,0:T(8,128)S(1)} %collective-permute-done.refs_1_), channel_id=1, source_target_pairs={{0,16},{8,24},{16,0},{24,8},{1,17},{9,25},{17,1},{25,9},{2,18},{10... | collective-permute-start | bytes 245768 | tf_op jit(solution)/shard_map/ppermute | solution.py:288
  21.8 1.9 %copy-start.7 = (f32[5,2,16,128]{3,2,1,0:T(8,128)}, f32[5,2,16,128]{3,2,1,0:T(8,128)S(1)}, u32[]{:S(2)}) copy-start(f32[5,2,16,128]{3,2,1,0:T(8,128)S(1)} %collective-permute-done.6.refs_7_) | copy-start | bytes 245764
  21.8 3.3 %collective-permute-start.1 = (f32[5,2,16,128]{3,2,1,0:T(8,128)S(1)}, f32[5,2,16,128]{3,2,1,0:T(8,128)S(1)}, u32[]{:S(2)}, u32[]{:S(2)}) collective-permute-start(f32[5,2,16,128]{3,2,1,0:T(8,128)S(1)} %collective-permute-done.refs_1_), channel_id=1, source_target_pairs={{0,8},{8,0},{16,24},{24,16},{1,9},{9,1},{17,25},{25,17},{2,10},{10... | collective-permute-start | bytes 245768 | tf_op jit(solution)/shard_map/ppermute | solution.py:288
  22.1 1.6 %copy-start.8 = (f32[5,2,16,128]{3,2,1,0:T(8,128)}, f32[5,2,16,128]{3,2,1,0:T(8,128)S(1)}, u32[]{:S(2)}) copy-start(f32[5,2,16,128]{3,2,1,0:T(8,128)S(1)} %collective-permute-done.5.refs_6_) | copy-start | bytes 245764
  22.1 6.9 %collective-permute-start.15 = (f32[4,5,2,16,128]{4,3,2,1,0:T(8,128)S(1)}, f32[4,5,2,16,128]{4,3,2,1,0:T(8,128)S(1)}, u32[]{:S(2)}, u32[]{:S(2)}) collective-permute-start(f32[4,5,2,16,128]{4,3,2,1,0:T(8,128)S(1)} %pad_maximum_fusion.2), channel_id=1, source_target_pairs={{0,1},{1,0},{2,3},{3,2},{4,5},{5,4},{6,7},{7,6},{8,9},{9,8},{10,11... | collective-permute-start | bytes 983048 | tf_op jit(solution)/shard_map/ppermute | solution.py:290
  23.7 5.3 %collective-permute-start.14 = (f32[4,5,2,16,128]{4,3,2,1,0:T(8,128)S(1)}, f32[4,5,2,16,128]{4,3,2,1,0:T(8,128)S(1)}, u32[]{:S(2)}, u32[]{:S(2)}) collective-permute-start(f32[4,5,2,16,128]{4,3,2,1,0:T(8,128)S(1)} %pad_maximum_fusion.1), channel_id=1, source_target_pairs={{0,1},{1,0},{2,3},{3,2},{4,5},{5,4},{6,7},{7,6},{8,9},{9,8},{10,11... | collective-permute-start | bytes 983048 | tf_op jit(solution)/shard_map/ppermute | solution.py:290
  25.7 3.9 %collective-permute-start.13 = (f32[4,5,2,16,128]{4,3,2,1,0:T(8,128)S(1)}, f32[4,5,2,16,128]{4,3,2,1,0:T(8,128)S(1)}, u32[]{:S(2)}, u32[]{:S(2)}) collective-permute-start(f32[4,5,2,16,128]{4,3,2,1,0:T(8,128)S(1)} %pad_maximum_fusion), channel_id=1, source_target_pairs={{0,1},{1,0},{2,3},{3,2},{4,5},{5,4},{6,7},{7,6},{8,9},{9,8},{10,11... | collective-permute-start | bytes 983048 | tf_op jit(solution)/shard_map/ppermute | solution.py:290
  (8 other events, 7.4 us)

commit v2 on v1

--- a/solution.py
+++ b/solution.py
@@ -46,7 +46,7 @@
     return high, low
 
 
-def levels_kernel(rows, n_near, n_far, where, *refs):
+def levels_kernel(rows, n_near, n_far, *refs):
     near, far = refs[:n_near], refs[n_near : n_near + n_far]
     refs = refs[n_near + n_far :]
     wz_first, wz_second, wy, wxy, out = refs[:5]
@@ -54,7 +54,7 @@
     fx, vis, part, G0, A1, A2, B1, A3, B2, C1, B3, C2, D1, C3, D2 = held
     fields, X, Y, Z = base.shape
     half = near[0].shape[2]
-    level, side = where[0], where[1]
+    level, side = lax.axis_index("level"), lax.axis_index("gy")
     own = (X - rows) // 2
 
     quarter = rows // 4
@@ -96,14 +96,14 @@
     def flux_rows(make, first, count, whole):
         batch = min(FLUX_ROWS, count)
 
-        def step(i, carry):
-            x = first + i * batch
+        def produce(x):
             u = [make(f, x, batch).reshape(batch * Y, Z) for f in range(fields)]
             along_x, along_y, along_z, g = pointwise(u)
             for f in range(fields):
                 fx[f, pl.ds(x + REACH, batch)] = along_x[f].reshape(batch, Y, Z)
             g = jnp.concatenate([v.astype(jnp.bfloat16) for v in g], axis=1)
-            vis[pl.ds(pl.multiple_of((x + REACH) * Y, Y), batch * Y), :] = g
+            at = (x + REACH) * Y
+            vis[pl.ds(at if isinstance(at, int) else pl.multiple_of(at, Y), batch * Y), :] = g
             if whole:
                 zs = [split(v) for v in along_z]
                 ys = [split(v) for v in along_y]
@@ -112,23 +112,38 @@
                 soft = jnp.concatenate([g[:, : 2 * Z], g[:, 2 * Z :]], axis=0)
                 soft = jnp.dot(soft, wz_second[...], preferred_element_type=jnp.float32)
                 group = wy.shape[0] // Y
+                deeps = []
                 for r in range(0, batch, group):
                     columns = []
                     for f in range(fields):
                         cuts = [slice((r + q) * Y, (r + q + 1) * Y) for q in range(group)]
                         columns.append(jnp.concatenate([v[cut] for cut in cuts for v in ys[f]], axis=0))
-                    deep = jnp.dot(wy[...], jnp.concatenate(columns, axis=1), preferred_element_type=jnp.float32)
-                    for f in range(fields):
-                        at = f * batch * Y + r * Y
-                        total = deep[:, f * Z : (f + 1) * Z] + flux[at : at + group * Y]
-                        if f:
-                            at = ((f - 1) // 2) * batch * Y + r * Y
-                            lane = ((f - 1) % 2) * Z
-                            total = total + soft[at : at + group * Y, lane : lane + Z]
-                        part[f, pl.ds(x + r, group)] = total.reshape(group, Y, Z)
+                    columns = jnp.concatenate(columns, axis=1)
+                    deeps.append(jnp.dot(wy[...], columns, preferred_element_type=jnp.float32))
+                return flux, soft, deeps
+            return None
+
+        def keep(x, flux, soft, deeps):
+            group = wy.shape[0] // Y
+            for r in range(0, batch, group):
+                deep = deeps[r // group]
+                for f in range(fields):
+                    at = f * batch * Y + r * Y
+                    total = deep[:, f * Z : (f + 1) * Z] + flux[at : at + group * Y]
+                    if f:
+                        at = ((f - 1) // 2) * batch * Y + r * Y
+                        lane = ((f - 1) % 2) * Z
+                        total = total + soft[at : at + group * Y, lane : lane + Z]
+                    part[f, pl.ds(x + r, group)] = total.reshape(group, Y, Z)
+
+        def step(i, carry):
+            made = [(x, produce(x)) for x in (first + i * count + j for j in range(0, count, batch))]
+            for x, values in made:
+                if values:
+                    keep(x, *values)
             return carry
 
-        lax.fori_loop(0, count // batch, step, 0)
+        lax.fori_loop(0, 1, step, 0)
 
     def stencil_rows(target, shift, first, count):
         block = wxy.shape[0] // Y
@@ -231,7 +246,7 @@
                 out[0, f] = total
 
 
-def run_levels(where, near, far, gx):
+def run_levels(near, far, gx):
     fields, rows, half, Z = near[0].shape
     X, Y = rows * gx, 2 * half
     bf16 = ml_dtypes.bfloat16
@@ -265,17 +280,16 @@
     return pl.pallas_call(
         functools.partial(levels_kernel, rows, len(near), len(far)),
         out_shape=jax.ShapeDtypeStruct((1, fields, rows, half, Z), jnp.float32),
-        in_specs=[pl.BlockSpec(memory_space=pltpu.SMEM)] + [vmem] * (len(near) + len(far) + 4),
+        in_specs=[vmem] * (len(near) + len(far) + 4),
         out_specs=vmem,
         scratch_shapes=scratch,
         compiler_params=pltpu.CompilerParams(vmem_limit_bytes=VMEM_BUDGET),
-    )(where, *near, *far, wz_first, wz_second, wy, wxy)
+    )(*near, *far, wz_first, wz_second, wy, wxy)
 
 
 def gathered_body(state):
     gx, levels = lax.axis_size("gx"), lax.axis_size("level")
     level = lax.axis_index("level")
-    where = jnp.stack([level, lax.axis_index("gy")]).astype(jnp.int32)
     swap = [(0, 1), (1, 0)]
     quarter = state.shape[1] // levels
     mine = lax.dynamic_slice_in_dim(state, level * quarter, quarter, axis=1)
@@ -288,7 +302,7 @@
             parts.append(lax.ppermute(first, "level", [(i, i ^ e) for i in range(levels)]))
         near += parts
         far.append(lax.ppermute(jnp.stack(parts), "gy", swap))
-    return run_levels(where, near, far, gx)
+    return run_levels(near, far, gx)
 
 
 def with_halo(block, sides, width):

time: 73.2 us -> 63.4 us (0.87)
  Pallas kernels: 42.4 us -> 33 us
    pallas_call x1, Pallas kernels: 42.4 us -> 33 us  [run_levels(): pl.pallas_call(functools.partial(levels_kernel, rows, len(near), len(far)...]
  transfers between devices with their start and end apart: 16 -> 16, of which waited for: 6 -> 6; matrix products, arithmetic and copies ran while one was open for 1% -> 0% of each run, Pallas kernels for 0% -> 0%
where the time goes in v2:
time: 63.4 us; the launch traced here: 63.3 us
  Pallas kernels  33 us (52%)
  starting transfers between devices  21.9 us (35%)
  waiting for transfers between devices  5.97 us (9%)
  local copies, waits for them, and re-layouts  2.24 us (4%)
    pallas_call x1, Pallas kernels, run_levels(): pl.pallas_call(functools.partial(levels_kernel, rows, len(near), len(far)...  33 us
    ppermute x9, starting transfers between devices, gathered_body(): lax.ppermute(first, 'level', [(i, i ^ e) for i in range(levels)])  8.1 us
    ppermute x1, starting transfers between devices, gathered_body(): near, far = ([state], [lax.ppermute(state, 'gy', swap)])  6.5 us
    ppermute x3, starting transfers between devices, gathered_body(): far.append(lax.ppermute(jnp.stack(parts), 'gy', swap))  4.7 us
    ppermute x9, waiting for transfers between devices, gathered_body(): lax.ppermute(first, 'level', [(i, i ^ e) for i in range(levels)])  3.5 us
    ppermute x3, starting transfers between devices, gathered_body(): first = lax.ppermute(mine, 'gx', route)  2.55 us
    unnamed x32, local copies, waits for them, and re-layouts  1.34 us
  transfers between devices with their start and end apart: 16, of which 6 were waited for; matrix products, arithmetic and copies ran while one was open for 0% of the time, Pallas kernels for 0%

profile of v2, /device:TPU:19, one launch (start us, length us, event | category | flops | bytes accessed | tf_op | source)
XLA Modules:
  0.0 63.3 jit_solution(3336492785325189543)
XLA Ops:
  0.0 0.9 %constant_dynamic-slice_fusion = f32[5,2,16,128]{3,2,1,0:T(8,128)S(1)} fusion(f32[5,8,16,128]{3,2,1,0:T(8,128)} %refs_0_.1, s32[]{:T(128)S(6)} %select_n.3), kind=kLoop, calls=%fused_computation.3 | loop fusion | bytes 163844 | tf_op jit(solution)/shard_map/dynamic_slice | solution.py:295
  0.9 1.3 %collective-permute-start.8 = (f32[5,2,16,128]{3,2,1,0:T(8,128)S(1)}, f32[5,2,16,128]{3,2,1,0:T(8,128)S(1)}, u32[]{:S(2)}, u32[]{:S(2)}) collective-permute-start(f32[5,2,16,128]{3,2,1,0:T(8,128)S(1)} %constant_dynamic-slice_fusion), channel_id=1, source_target_pairs={{6,0},{0,2},{2,4},{4,6},{7,1},{1,3},{3,5},{5,7},{14,8},{8,10},{10,... | collective-permute-start | bytes 245768 | tf_op jit(solution)/shard_map/ppermute | solution.py:299
  2.2 1.2 %collective-permute-start = (f32[5,2,16,128]{3,2,1,0:T(8,128)S(1)}, f32[5,2,16,128]{3,2,1,0:T(8,128)S(1)}, u32[]{:S(2)}, u32[]{:S(2)}) collective-permute-start(f32[5,2,16,128]{3,2,1,0:T(8,128)S(1)} %constant_dynamic-slice_fusion), channel_id=1, source_target_pairs={{2,0},{4,2},{6,4},{0,6},{3,1},{5,3},{7,5},{1,7},{10,8},{12,10},{14... | collective-permute-start | bytes 245768 | tf_op jit(solution)/shard_map/ppermute | solution.py:299
  3.4 0.7 %collective-permute-done.8.refs_9_ = f32[5,2,16,128]{3,2,1,0:T(8,128)S(1)} collective-permute-done((f32[5,2,16,128]{3,2,1,0:T(8,128)S(1)}, f32[5,2,16,128]{3,2,1,0:T(8,128)S(1)}, u32[]{:S(2)}, u32[]{:S(2)}) %collective-permute-start.8) | collective-permute-done | bytes 81952 | tf_op jit(solution)/shard_map/ppermute | solution.py:299
  4.2 1.2 %collective-permute-start.11 = (f32[5,2,16,128]{3,2,1,0:T(8,128)S(1)}, f32[5,2,16,128]{3,2,1,0:T(8,128)S(1)}, u32[]{:S(2)}, u32[]{:S(2)}) collective-permute-start(f32[5,2,16,128]{3,2,1,0:T(8,128)S(1)} %collective-permute-done.8.refs_9_), channel_id=1, source_target_pairs={{0,24},{8,16},{16,8},{24,0},{1,25},{9,17},{17,9},{25,1},{2,26},{10... | collective-permute-start | bytes 245768 | tf_op jit(solution)/shard_map/ppermute | solution.py:302
  5.6 1.2 %collective-permute-start.9 = (f32[5,2,16,128]{3,2,1,0:T(8,128)S(1)}, f32[5,2,16,128]{3,2,1,0:T(8,128)S(1)}, u32[]{:S(2)}, u32[]{:S(2)}) collective-permute-start(f32[5,2,16,128]{3,2,1,0:T(8,128)S(1)} %collective-permute-done.8.refs_9_), channel_id=1, source_target_pairs={{0,8},{8,0},{16,24},{24,16},{1,9},{9,1},{17,25},{25,17},{2,10},{10... | collective-permute-start | bytes 245768 | tf_op jit(solution)/shard_map/ppermute | solution.py:302
  6.8 0.5 collective-permute-done.4.refs_5_
  7.3 6.5 %collective-permute-start.12 = (f32[5,8,16,128]{3,2,1,0:T(8,128)}, f32[5,8,16,128]{3,2,1,0:T(8,128)S(1)}, u32[]{:S(2)}, u32[]{:S(2)}) collective-permute-start(f32[5,8,16,128]{3,2,1,0:T(8,128)} %refs_0_.1), channel_id=1, source_target_pairs={{0,1},{1,0},{2,3},{3,2},{4,5},{5,4},{6,7},{7,6},{8,9},{9,8},{10,11... | collective-permute-start | bytes 983048 | tf_op jit(solution)/shard_map/ppermute | solution.py:296
  13.9 1.2 %collective-permute-start.7 = (f32[5,2,16,128]{3,2,1,0:T(8,128)S(1)}, f32[5,2,16,128]{3,2,1,0:T(8,128)S(1)}, u32[]{:S(2)}, u32[]{:S(2)}) collective-permute-start(f32[5,2,16,128]{3,2,1,0:T(8,128)S(1)} %collective-permute-done.4.refs_5_), channel_id=1, source_target_pairs={{0,24},{8,16},{16,8},{24,0},{1,25},{9,17},{17,9},{25,1},{2,26},{10... | collective-permute-start | bytes 245768 | tf_op jit(solution)/shard_map/ppermute | solution.py:302
  15.1 0.2 collective-permute-start.6
  15.3 1.2 %collective-permute-start.5 = (f32[5,2,16,128]{3,2,1,0:T(8,128)S(1)}, f32[5,2,16,128]{3,2,1,0:T(8,128)S(1)}, u32[]{:S(2)}, u32[]{:S(2)}) collective-permute-start(f32[5,2,16,128]{3,2,1,0:T(8,128)S(1)} %collective-permute-done.4.refs_5_), channel_id=1, source_target_pairs={{0,8},{8,0},{16,24},{24,16},{1,9},{9,1},{17,25},{25,17},{2,10},{10... | collective-permute-start | bytes 245768 | tf_op jit(solution)/shard_map/ppermute | solution.py:302
  16.5 1.2 %collective-permute-start.3 = (f32[5,2,16,128]{3,2,1,0:T(8,128)S(1)}, f32[5,2,16,128]{3,2,1,0:T(8,128)S(1)}, u32[]{:S(2)}, u32[]{:S(2)}) collective-permute-start(f32[5,2,16,128]{3,2,1,0:T(8,128)S(1)} %collective-permute-done.refs_1_), channel_id=1, source_target_pairs={{0,24},{8,16},{16,8},{24,0},{1,25},{9,17},{17,9},{25,1},{2,26},{10... | collective-permute-start | bytes 245768 | tf_op jit(solution)/shard_map/ppermute | solution.py:302
  17.8 1.0 %collective-permute-done.7.refs_8_ = f32[5,2,16,128]{3,2,1,0:T(8,128)S(1)} collective-permute-done((f32[5,2,16,128]{3,2,1,0:T(8,128)S(1)}, f32[5,2,16,128]{3,2,1,0:T(8,128)S(1)}, u32[]{:S(2)}, u32[]{:S(2)}) %collective-permute-start.7) | collective-permute-done | bytes 81952 | tf_op jit(solution)/shard_map/ppermute | solution.py:302
  18.8 1.3 %collective-permute-start.2 = (f32[5,2,16,128]{3,2,1,0:T(8,128)S(1)}, f32[5,2,16,128]{3,2,1,0:T(8,128)S(1)}, u32[]{:S(2)}, u32[]{:S(2)}) collective-permute-start(f32[5,2,16,128]{3,2,1,0:T(8,128)S(1)} %collective-permute-done.refs_1_), channel_id=1, source_target_pairs={{0,16},{8,24},{16,0},{24,8},{1,17},{9,25},{17,1},{25,9},{2,18},{10... | collective-permute-start | bytes 245768 | tf_op jit(solution)/shard_map/ppermute | solution.py:302
  20.1 1.7 %collective-permute-done.6.refs_7_ = f32[5,2,16,128]{3,2,1,0:T(8,128)S(1)} collective-permute-done((f32[5,2,16,128]{3,2,1,0:T(8,128)S(1)}, f32[5,2,16,128]{3,2,1,0:T(8,128)S(1)}, u32[]{:S(2)}, u32[]{:S(2)}) %collective-permute-start.6) | collective-permute-done | bytes 81952 | tf_op jit(solution)/shard_map/ppermute | solution.py:302
  21.8 0.3 collective-permute-start.1
  22.1 1.5 %collective-permute-start.15 = (f32[4,5,2,16,128]{4,3,2,1,0:T(8,128)S(1)}, f32[4,5,2,16,128]{4,3,2,1,0:T(8,128)S(1)}, u32[]{:S(2)}, u32[]{:S(2)}) collective-permute-start(f32[4,5,2,16,128]{4,3,2,1,0:T(8,128)S(1)} %pad_maximum_fusion.2), channel_id=1, source_target_pairs={{0,1},{1,0},{2,3},{3,2},{4,5},{5,4},{6,7},{7,6},{8,9},{9,8},{10,11... | collective-permute-start | bytes 983048 | tf_op jit(solution)/shard_map/ppermute | solution.py:304
  23.7 0.6 collective-permute-start.14
  24.2 0.8 %collective-permute-done.1.refs_2_ = f32[5,2,16,128]{3,2,1,0:T(8,128)S(1)} collective-permute-done((f32[5,2,16,128]{3,2,1,0:T(8,128)S(1)}, f32[5,2,16,128]{3,2,1,0:T(8,128)S(1)}, u32[]{:S(2)}, u32[]{:S(2)}) %collective-permute-start.1) | collective-permute-done | bytes 81952 | tf_op jit(solution)/shard_map/ppermute | solution.py:302
  25.1 0.6 copy-done.15
  25.7 2.6 %collective-permute-start.13 = (f32[4,5,2,16,128]{4,3,2,1,0:T(8,128)S(1)}, f32[4,5,2,16,128]{4,3,2,1,0:T(8,128)S(1)}, u32[]{:S(2)}, u32[]{:S(2)}) collective-permute-start(f32[4,5,2,16,128]{4,3,2,1,0:T(8,128)S(1)} %pad_maximum_fusion), channel_id=1, source_target_pairs={{0,1},{1,0},{2,3},{3,2},{4,5},{5,4},{6,7},{7,6},{8,9},{9,8},{10,11... | collective-permute-start | bytes 983048 | tf_op jit(solution)/shard_map/ppermute | solution.py:304
  28.3 1.2 %collective-permute-done.13.refs_14_ = f32[4,5,2,16,128]{4,3,2,1,0:T(8,128)S(1)} collective-permute-done((f32[4,5,2,16,128]{4,3,2,1,0:T(8,128)S(1)}, f32[4,5,2,16,128]{4,3,2,1,0:T(8,128)S(1)}, u32[]{:S(2)}, u32[]{:S(2)}) %collective-permute-start.13) | collective-permute-done | bytes 327712 | tf_op jit(solution)/shard_map/ppermute | solution.py:304
  29.6 0.7 %copy-done.3 = f32[4,5,2,16,128]{4,3,2,1,0:T(8,128)} copy-done((f32[4,5,2,16,128]{4,3,2,1,0:T(8,128)}, f32[4,5,2,16,128]{4,3,2,1,0:T(8,128)S(1)}, u32[]{:S(2)}) %copy-start.3) | copy-done | bytes 327704
  30.3 33.0 %shard_map.55 = f32[1,5,8,16,128]{4,3,2,1,0:T(8,128)} custom-call(f32[5,8,16,128]{3,2,1,0:T(8,128)} %refs_0_.1, f32[5,2,16,128]{3,2,1,0:T(8,128)} %copy-done.6, f32[5,2,16,128]{3,2,1,0:T(8,128)} %copy-done.15, f32[5,2,16,128]{3,2,1,0:T(8,128)} %copy-done.14, f32[5,2,16,128]{3,2,1,0:T(8,128)} %copy-done.13, f32[5,2,16,128]{3,2,1,0:T(8,128)} %copy-done.5, ...), custom_call_target="tpu_custom_call" | custom-call | tf_op jit(solution)/shard_map/pallas_call | solution.py:280
  (45 shorter events, 0.4 us)
Async XLA Ops:
  0.9 3.3 %collective-permute-start.8 = (f32[5,2,16,128]{3,2,1,0:T(8,128)S(1)}, f32[5,2,16,128]{3,2,1,0:T(8,128)S(1)}, u32[]{:S(2)}, u32[]{:S(2)}) collective-permute-start(f32[5,2,16,128]{3,2,1,0:T(8,128)S(1)} %constant_dynamic-slice_fusion), channel_id=1, source_target_pairs={{6,0},{0,2},{2,4},{4,6},{7,1},{1,3},{3,5},{5,7},{14,8},{8,10},{10,... | collective-permute-start | bytes 245768 | tf_op jit(solution)/shard_map/ppermute | solution.py:299
  2.2 5.2 %collective-permute-start.4 = (f32[5,2,16,128]{3,2,1,0:T(8,128)S(1)}, f32[5,2,16,128]{3,2,1,0:T(8,128)S(1)}, u32[]{:S(2)}, u32[]{:S(2)}) collective-permute-start(f32[5,2,16,128]{3,2,1,0:T(8,128)S(1)} %constant_dynamic-slice_fusion), channel_id=1, source_target_pairs={{4,0},{6,2},{0,4},{2,6},{5,1},{7,3},{1,5},{3,7},{12,8},{14,10},{8,... | collective-permute-start | bytes 245768 | tf_op jit(solution)/shard_map/ppermute | solution.py:299
  2.2 11.6 %collective-permute-start = (f32[5,2,16,128]{3,2,1,0:T(8,128)S(1)}, f32[5,2,16,128]{3,2,1,0:T(8,128)S(1)}, u32[]{:S(2)}, u32[]{:S(2)}) collective-permute-start(f32[5,2,16,128]{3,2,1,0:T(8,128)S(1)} %constant_dynamic-slice_fusion), channel_id=1, source_target_pairs={{2,0},{4,2},{6,4},{0,6},{3,1},{5,3},{7,5},{1,7},{10,8},{12,10},{14... | collective-permute-start | bytes 245768 | tf_op jit(solution)/shard_map/ppermute | solution.py:299
  4.2 13.6 %copy-start.4 = (f32[5,2,16,128]{3,2,1,0:T(8,128)}, f32[5,2,16,128]{3,2,1,0:T(8,128)S(1)}, u32[]{:S(2)}) copy-start(f32[5,2,16,128]{3,2,1,0:T(8,128)S(1)} %collective-permute-done.8.refs_9_) | copy-start | bytes 245764
  4.2 10.9 %collective-permute-start.11 = (f32[5,2,16,128]{3,2,1,0:T(8,128)S(1)}, f32[5,2,16,128]{3,2,1,0:T(8,128)S(1)}, u32[]{:S(2)}, u32[]{:S(2)}) collective-permute-start(f32[5,2,16,128]{3,2,1,0:T(8,128)S(1)} %collective-permute-done.8.refs_9_), channel_id=1, source_target_pairs={{0,24},{8,16},{16,8},{24,0},{1,25},{9,17},{17,9},{25,1},{2,26},{10... | collective-permute-start | bytes 245768 | tf_op jit(solution)/shard_map/ppermute | solution.py:302
  5.4 9.9 %collective-permute-start.10 = (f32[5,2,16,128]{3,2,1,0:T(8,128)S(1)}, f32[5,2,16,128]{3,2,1,0:T(8,128)S(1)}, u32[]{:S(2)}, u32[]{:S(2)}) collective-permute-start(f32[5,2,16,128]{3,2,1,0:T(8,128)S(1)} %collective-permute-done.8.refs_9_), channel_id=1, source_target_pairs={{0,16},{8,24},{16,0},{24,8},{1,17},{9,25},{17,1},{25,9},{2,18},{10... | collective-permute-start | bytes 245768 | tf_op jit(solution)/shard_map/ppermute | solution.py:302
  5.6 10.9 %collective-permute-start.9 = (f32[5,2,16,128]{3,2,1,0:T(8,128)S(1)}, f32[5,2,16,128]{3,2,1,0:T(8,128)S(1)}, u32[]{:S(2)}, u32[]{:S(2)}) collective-permute-start(f32[5,2,16,128]{3,2,1,0:T(8,128)S(1)} %collective-permute-done.8.refs_9_), channel_id=1, source_target_pairs={{0,8},{8,0},{16,24},{24,16},{1,9},{9,1},{17,25},{25,17},{2,10},{10... | collective-permute-start | bytes 245768 | tf_op jit(solution)/shard_map/ppermute | solution.py:302
  7.3 16.3 %copy-start.5 = (f32[5,2,16,128]{3,2,1,0:T(8,128)}, f32[5,2,16,128]{3,2,1,0:T(8,128)S(1)}, u32[]{:S(2)}) copy-start(f32[5,2,16,128]{3,2,1,0:T(8,128)S(1)} %collective-permute-done.4.refs_5_) | copy-start | bytes 245764
  7.3 21.0 %collective-permute-start.12 = (f32[5,8,16,128]{3,2,1,0:T(8,128)}, f32[5,8,16,128]{3,2,1,0:T(8,128)S(1)}, u32[]{:S(2)}, u32[]{:S(2)}) collective-permute-start(f32[5,8,16,128]{3,2,1,0:T(8,128)} %refs_0_.1), channel_id=1, source_target_pairs={{0,1},{1,0},{2,3},{3,2},{4,5},{5,4},{6,7},{7,6},{8,9},{9,8},{10,11... | collective-permute-start | bytes 983048 | tf_op jit(solution)/shard_map/ppermute | solution.py:296
  13.8 11.2 %copy-start.6 = (f32[5,2,16,128]{3,2,1,0:T(8,128)}, f32[5,2,16,128]{3,2,1,0:T(8,128)S(1)}, u32[]{:S(2)}) copy-start(f32[5,2,16,128]{3,2,1,0:T(8,128)S(1)} %collective-permute-done.refs_1_) | copy-start | bytes 245764
  13.9 4.9 %collective-permute-start.7 = (f32[5,2,16,128]{3,2,1,0:T(8,128)S(1)}, f32[5,2,16,128]{3,2,1,0:T(8,128)S(1)}, u32[]{:S(2)}, u32[]{:S(2)}) collective-permute-start(f32[5,2,16,128]{3,2,1,0:T(8,128)S(1)} %collective-permute-done.4.refs_5_), channel_id=1, source_target_pairs={{0,24},{8,16},{16,8},{24,0},{1,25},{9,17},{17,9},{25,1},{2,26},{10... | collective-permute-start | bytes 245768 | tf_op jit(solution)/shard_map/ppermute | solution.py:302
  15.1 2.7 %copy-start.7 = (f32[5,2,16,128]{3,2,1,0:T(8,128)}, f32[5,2,16,128]{3,2,1,0:T(8,128)S(1)}, u32[]{:S(2)}) copy-start(f32[5,2,16,128]{3,2,1,0:T(8,128)S(1)} %collective-permute-done.11.refs_12_) | copy-start | bytes 245764
  15.1 6.7 %collective-permute-start.6 = (f32[5,2,16,128]{3,2,1,0:T(8,128)S(1)}, f32[5,2,16,128]{3,2,1,0:T(8,128)S(1)}, u32[]{:S(2)}, u32[]{:S(2)}) collective-permute-start(f32[5,2,16,128]{3,2,1,0:T(8,128)S(1)} %collective-permute-done.4.refs_5_), channel_id=1, source_target_pairs={{0,16},{8,24},{16,0},{24,8},{1,17},{9,25},{17,1},{25,9},{2,18},{10... | collective-permute-start | bytes 245768 | tf_op jit(solution)/shard_map/ppermute | solution.py:302
  15.3 2.5 %copy-start.8 = (f32[5,2,16,128]{3,2,1,0:T(8,128)}, f32[5,2,16,128]{3,2,1,0:T(8,128)S(1)}, u32[]{:S(2)}) copy-start(f32[5,2,16,128]{3,2,1,0:T(8,128)S(1)} %collective-permute-done.10.refs_11_) | copy-start | bytes 245764
  15.3 6.7 %collective-permute-start.5 = (f32[5,2,16,128]{3,2,1,0:T(8,128)S(1)}, f32[5,2,16,128]{3,2,1,0:T(8,128)S(1)}, u32[]{:S(2)}, u32[]{:S(2)}) collective-permute-start(f32[5,2,16,128]{3,2,1,0:T(8,128)S(1)} %collective-permute-done.4.refs_5_), channel_id=1, source_target_pairs={{0,8},{8,0},{16,24},{24,16},{1,9},{9,1},{17,25},{25,17},{2,10},{10... | collective-permute-start | bytes 245768 | tf_op jit(solution)/shard_map/ppermute | solution.py:302
  16.5 7.1 %collective-permute-start.3 = (f32[5,2,16,128]{3,2,1,0:T(8,128)S(1)}, f32[5,2,16,128]{3,2,1,0:T(8,128)S(1)}, u32[]{:S(2)}, u32[]{:S(2)}) collective-permute-start(f32[5,2,16,128]{3,2,1,0:T(8,128)S(1)} %collective-permute-done.refs_1_), channel_id=1, source_target_pairs={{0,24},{8,16},{16,8},{24,0},{1,25},{9,17},{17,9},{25,1},{2,26},{10... | collective-permute-start | bytes 245768 | tf_op jit(solution)/shard_map/ppermute | solution.py:302
  18.8 4.9 %copy-start.10 = (f32[5,2,16,128]{3,2,1,0:T(8,128)}, f32[5,2,16,128]{3,2,1,0:T(8,128)S(1)}, u32[]{:S(2)}) copy-start(f32[5,2,16,128]{3,2,1,0:T(8,128)S(1)} %collective-permute-done.7.refs_8_) | copy-start | bytes 245764
  18.8 5.5 %collective-permute-start.2 = (f32[5,2,16,128]{3,2,1,0:T(8,128)S(1)}, f32[5,2,16,128]{3,2,1,0:T(8,128)S(1)}, u32[]{:S(2)}, u32[]{:S(2)}) collective-permute-start(f32[5,2,16,128]{3,2,1,0:T(8,128)S(1)} %collective-permute-done.refs_1_), channel_id=1, source_target_pairs={{0,16},{8,24},{16,0},{24,8},{1,17},{9,25},{17,1},{25,9},{2,18},{10... | collective-permute-start | bytes 245768 | tf_op jit(solution)/shard_map/ppermute | solution.py:302
  21.8 1.9 %copy-start.11 = (f32[5,2,16,128]{3,2,1,0:T(8,128)}, f32[5,2,16,128]{3,2,1,0:T(8,128)S(1)}, u32[]{:S(2)}) copy-start(f32[5,2,16,128]{3,2,1,0:T(8,128)S(1)} %collective-permute-done.6.refs_7_) | copy-start | bytes 245764
  21.8 3.3 %collective-permute-start.1 = (f32[5,2,16,128]{3,2,1,0:T(8,128)S(1)}, f32[5,2,16,128]{3,2,1,0:T(8,128)S(1)}, u32[]{:S(2)}, u32[]{:S(2)}) collective-permute-start(f32[5,2,16,128]{3,2,1,0:T(8,128)S(1)} %collective-permute-done.refs_1_), channel_id=1, source_target_pairs={{0,8},{8,0},{16,24},{24,16},{1,9},{9,1},{17,25},{25,17},{2,10},{10... | collective-permute-start | bytes 245768 | tf_op jit(solution)/shard_map/ppermute | solution.py:302
  22.1 1.6 %copy-start.12 = (f32[5,2,16,128]{3,2,1,0:T(8,128)}, f32[5,2,16,128]{3,2,1,0:T(8,128)S(1)}, u32[]{:S(2)}) copy-start(f32[5,2,16,128]{3,2,1,0:T(8,128)S(1)} %collective-permute-done.5.refs_6_) | copy-start | bytes 245764
  22.1 6.2 %collective-permute-start.15 = (f32[4,5,2,16,128]{4,3,2,1,0:T(8,128)S(1)}, f32[4,5,2,16,128]{4,3,2,1,0:T(8,128)S(1)}, u32[]{:S(2)}, u32[]{:S(2)}) collective-permute-start(f32[4,5,2,16,128]{4,3,2,1,0:T(8,128)S(1)} %pad_maximum_fusion.2), channel_id=1, source_target_pairs={{0,1},{1,0},{2,3},{3,2},{4,5},{5,4},{6,7},{7,6},{8,9},{9,8},{10,11... | collective-permute-start | bytes 983048 | tf_op jit(solution)/shard_map/ppermute | solution.py:304
  23.7 4.6 %collective-permute-start.14 = (f32[4,5,2,16,128]{4,3,2,1,0:T(8,128)S(1)}, f32[4,5,2,16,128]{4,3,2,1,0:T(8,128)S(1)}, u32[]{:S(2)}, u32[]{:S(2)}) collective-permute-start(f32[4,5,2,16,128]{4,3,2,1,0:T(8,128)S(1)} %pad_maximum_fusion.1), channel_id=1, source_target_pairs={{0,1},{1,0},{2,3},{3,2},{4,5},{5,4},{6,7},{7,6},{8,9},{9,8},{10,11... | collective-permute-start | bytes 983048 | tf_op jit(solution)/shard_map/ppermute | solution.py:304
  25.7 3.9 %collective-permute-start.13 = (f32[4,5,2,16,128]{4,3,2,1,0:T(8,128)S(1)}, f32[4,5,2,16,128]{4,3,2,1,0:T(8,128)S(1)}, u32[]{:S(2)}, u32[]{:S(2)}) collective-permute-start(f32[4,5,2,16,128]{4,3,2,1,0:T(8,128)S(1)} %pad_maximum_fusion), channel_id=1, source_target_pairs={{0,1},{1,0},{2,3},{3,2},{4,5},{5,4},{6,7},{7,6},{8,9},{9,8},{10,11... | collective-permute-start | bytes 983048 | tf_op jit(solution)/shard_map/ppermute | solution.py:304
  (8 other events, 8.6 us)

commit v3 on v2

--- a/solution.py
+++ b/solution.py
@@ -46,6 +46,10 @@
     return high, low
 
 
+def far_first(count):
+    return sorted(range(1, count), key=lambda ahead: (-min(ahead, count - ahead), -ahead))
+
+
 def levels_kernel(rows, n_near, n_far, *refs):
     near, far = refs[:n_near], refs[n_near : n_near + n_far]
     refs = refs[n_near + n_far :]
@@ -71,10 +75,10 @@
 
     lay(near[0][...], side, 0, None)
     lay(far[0][...], 1 - side, 0, None)
-    for ahead in range(1, X // rows):
-        for e in range(4):
-            lay(near[4 * ahead - 3 + e][...], side, ahead, e)
-            lay(far[ahead][e], 1 - side, ahead, e)
+    for e in range(4):
+        for j, ahead in enumerate(far_first(X // rows)):
+            lay(near[1 + e][j], side, ahead, e)
+            lay(far[1 + e][j], 1 - side, ahead, e)
 
     def pointwise(u):
         rho, m0, m1, m2, energy = u
@@ -293,15 +297,17 @@
     swap = [(0, 1), (1, 0)]
     quarter = state.shape[1] // levels
     mine = lax.dynamic_slice_in_dim(state, level * quarter, quarter, axis=1)
-    near, far = [state], [lax.ppermute(state, "gy", swap)]
-    for ahead in range(1, gx):
-        route = [((i + ahead) % gx, i) for i in range(gx)]
-        first = lax.ppermute(mine, "gx", route)
-        parts = [first]
-        for e in range(1, levels):
-            parts.append(lax.ppermute(first, "level", [(i, i ^ e) for i in range(levels)]))
-        near += parts
-        far.append(lax.ppermute(jnp.stack(parts), "gy", swap))
+    far = [lax.ppermute(state, "gy", swap)]
+    first = []
+    for ahead in far_first(gx):
+        first.append(lax.ppermute(mine, "gx", [((i + ahead) % gx, i) for i in range(gx)]))
+    first = jnp.stack(first)
+    parts = {0: first}
+    for e in range(levels - 1, 0, -1):
+        parts[e] = lax.ppermute(first, "level", [(i, i ^ e) for i in range(levels)])
+    swapped = {e: lax.ppermute(part, "gy", swap) for e, part in parts.items()}
+    near = [state] + [parts[e] for e in range(levels)]
+    far += [swapped[e] for e in range(levels)]
     return run_levels(near, far, gx)
 
 

time: 63.4 us -> 61.3 us (0.967)
  the two profiles are of different devices: /device:TPU:19 before, /device:TPU:29 now
where the time goes in v3:
time: 61.3 us; the launch traced here: 61.2 us
  Pallas kernels  33 us (54%)
  waiting for transfers between devices  14.1 us (23%)
  starting transfers between devices  12 us (20%)
  local copies, waits for them, and re-layouts  1.98 us (3%)
    pallas_call x1, Pallas kernels, run_levels(): pl.pallas_call(functools.partial(levels_kernel, rows, len(near), len(far)...  33 us
    ppermute x3, waiting for transfers between devices, gathered_body(): lax.ppermute(mine, 'gx', [((i + ahead) % gx, i) for i in range(gx)])  6.73 us
    ppermute x3, waiting for transfers between devices, gathered_body(): parts[e] = lax.ppermute(first, 'level', [(i, i ^ e) for i in range(levels)])  5.97 us
    ppermute x4, starting transfers between devices, gathered_body(): swapped = {e: lax.ppermute(part, 'gy', swap) for e, part in parts.items()}  4.1 us
    ppermute x3, starting transfers between devices, gathered_body(): lax.ppermute(mine, 'gx', [((i + ahead) % gx, i) for i in range(gx)])  3.27 us
    ppermute x3, starting transfers between devices, gathered_body(): parts[e] = lax.ppermute(first, 'level', [(i, i ^ e) for i in range(levels)])  2.71 us
    ppermute x1, starting transfers between devices, gathered_body(): far = [lax.ppermute(state, 'gy', swap)]  1.88 us
    ppermute x4, waiting for transfers between devices, gathered_body(): swapped = {e: lax.ppermute(part, 'gy', swap) for e, part in parts.items()}  1.39 us
  transfers between devices with their start and end apart: 11, of which 6 were waited for; matrix products, arithmetic and copies ran while one was open for 0% of the time, Pallas kernels for 0%

profile of v3, /device:TPU:29, one launch (start us, length us, event | category | flops | bytes accessed | tf_op | source)
XLA Modules:
  0.0 61.2 jit_solution(7481826955230647440)
XLA Ops:
  0.0 1.0 %constant_dynamic-slice_fusion = f32[5,2,16,128]{3,2,1,0:T(8,128)S(1)} fusion(f32[5,8,16,128]{3,2,1,0:T(8,128)} %refs_0_.1, s32[]{:T(128)S(6)} %select_n.3), kind=kLoop, calls=%fused_computation.1 | loop fusion | bytes 163844 | tf_op jit(solution)/shard_map/dynamic_slice | solution.py:299
  1.0 0.2 collective-permute-start.2
  1.1 3.1 %collective-permute-start.1 = (f32[5,2,16,128]{3,2,1,0:T(8,128)S(1)}, f32[5,2,16,128]{3,2,1,0:T(8,128)S(1)}, u32[]{:S(2)}, u32[]{:S(2)}) collective-permute-start(f32[5,2,16,128]{3,2,1,0:T(8,128)S(1)} %constant_dynamic-slice_fusion), channel_id=1, source_target_pairs={{6,0},{0,2},{2,4},{4,6},{7,1},{1,3},{3,5},{5,7},{14,8},{8,10},{10,... | collective-permute-start | bytes 245768 | tf_op jit(solution)/shard_map/ppermute | solution.py:303
  4.2 2.0 %collective-permute-done.2 = f32[5,2,16,128]{3,2,1,0:T(8,128)S(1)} collective-permute-done((f32[5,2,16,128]{3,2,1,0:T(8,128)S(1)}, f32[5,2,16,128]{3,2,1,0:T(8,128)S(1)}, u32[]{:S(2)}, u32[]{:S(2)}) %collective-permute-start.2) | collective-permute-done | bytes 81952 | tf_op jit(solution)/shard_map/ppermute | solution.py:303
  6.2 0.0 collective-permute-done.1
  6.2 4.8 %collective-permute-done = f32[5,2,16,128]{3,2,1,0:T(8,128)S(1)} collective-permute-done((f32[5,2,16,128]{3,2,1,0:T(8,128)S(1)}, f32[5,2,16,128]{3,2,1,0:T(8,128)S(1)}, u32[]{:S(2)}, u32[]{:S(2)}) %collective-permute-start) | collective-permute-done | bytes 81952 | tf_op jit(solution)/shard_map/ppermute | solution.py:303
  11.0 1.2 %collective-permute-start.5 = (f32[3,5,2,16,128]{4,3,2,1,0:T(8,128)S(1)}, f32[3,5,2,16,128]{4,3,2,1,0:T(8,128)S(1)}, u32[]{:S(2)}, u32[]{:S(2)}) collective-permute-start(f32[3,5,2,16,128]{4,3,2,1,0:T(8,128)S(1)} %pad_maximum_fusion.refs_1_), channel_id=1, source_target_pairs={{0,24},{8,16},{16,8},{24,0},{1,25},{9,17},{17,9},{25,1},{2,26},{10... | collective-permute-start | bytes 737288 | tf_op jit(solution)/shard_map/ppermute | solution.py:307
  12.2 1.2 %collective-permute-start.4 = (f32[3,5,2,16,128]{4,3,2,1,0:T(8,128)S(1)}, f32[3,5,2,16,128]{4,3,2,1,0:T(8,128)S(1)}, u32[]{:S(2)}, u32[]{:S(2)}) collective-permute-start(f32[3,5,2,16,128]{4,3,2,1,0:T(8,128)S(1)} %pad_maximum_fusion.refs_1_), channel_id=1, source_target_pairs={{0,16},{8,24},{16,0},{24,8},{1,17},{9,25},{17,1},{25,9},{2,18},{10... | collective-permute-start | bytes 737288 | tf_op jit(solution)/shard_map/ppermute | solution.py:307
  13.5 0.3 collective-permute-start.3
  13.7 1.9 %collective-permute-start.6 = (f32[5,8,16,128]{3,2,1,0:T(8,128)S(1)}, f32[5,8,16,128]{3,2,1,0:T(8,128)S(1)}, u32[]{:S(2)}, u32[]{:S(2)}) collective-permute-start(f32[5,8,16,128]{3,2,1,0:T(8,128)S(1)} %copy-done.1), channel_id=1, source_target_pairs={{0,1},{1,0},{2,3},{3,2},{4,5},{5,4},{6,7},{7,6},{8,9},{9,8},{10,11... | collective-permute-start | bytes 983048 | tf_op jit(solution)/shard_map/ppermute | solution.py:300
  15.6 0.0 collective-permute-start.7
  15.6 2.8 %collective-permute-done.5.refs_4_ = f32[3,5,2,16,128]{4,3,2,1,0:T(8,128)S(1)} collective-permute-done((f32[3,5,2,16,128]{4,3,2,1,0:T(8,128)S(1)}, f32[3,5,2,16,128]{4,3,2,1,0:T(8,128)S(1)}, u32[]{:S(2)}, u32[]{:S(2)}) %collective-permute-start.5) | collective-permute-done | bytes 245792 | tf_op jit(solution)/shard_map/ppermute | solution.py:307
  18.4 3.5 %collective-permute-start.10 = (f32[3,5,2,16,128]{4,3,2,1,0:T(8,128)S(1)}, f32[3,5,2,16,128]{4,3,2,1,0:T(8,128)S(1)}, u32[]{:S(2)}, u32[]{:S(2)}) collective-permute-start(f32[3,5,2,16,128]{4,3,2,1,0:T(8,128)S(1)} %collective-permute-done.5.refs_4_), channel_id=1, source_target_pairs={{0,1},{1,0},{2,3},{3,2},{4,5},{5,4},{6,7},{7,6},{8,9},{9,8},{10,11... | collective-permute-start | bytes 737288 | tf_op jit(solution)/shard_map/ppermute | solution.py:308
  21.9 3.2 %collective-permute-done.4.refs_3_ = f32[3,5,2,16,128]{4,3,2,1,0:T(8,128)S(1)} collective-permute-done((f32[3,5,2,16,128]{4,3,2,1,0:T(8,128)S(1)}, f32[3,5,2,16,128]{4,3,2,1,0:T(8,128)S(1)}, u32[]{:S(2)}, u32[]{:S(2)}) %collective-permute-start.4) | collective-permute-done | bytes 245792 | tf_op jit(solution)/shard_map/ppermute | solution.py:307
  25.1 0.5 collective-permute-start.9
  25.6 0.0 collective-permute-done.3.refs_2_
  25.6 0.1 collective-permute-start.8
  25.7 0.0 collective-permute-done.6.refs_5_
  25.7 0.0 collective-permute-done.10.refs_9_
  25.7 1.0 %collective-permute-done.9.refs_8_ = f32[3,5,2,16,128]{4,3,2,1,0:T(8,128)S(1)} collective-permute-done((f32[3,5,2,16,128]{4,3,2,1,0:T(8,128)S(1)}, f32[3,5,2,16,128]{4,3,2,1,0:T(8,128)S(1)}, u32[]{:S(2)}, u32[]{:S(2)}) %collective-permute-start.9) | collective-permute-done | bytes 245792 | tf_op jit(solution)/shard_map/ppermute | solution.py:308
  26.7 0.4 collective-permute-done.8.refs_7_
  27.2 0.3 copy-done.8
  27.5 0.7 %copy-done.9 = f32[3,5,2,16,128]{4,3,2,1,0:T(8,128)} copy-done((f32[3,5,2,16,128]{4,3,2,1,0:T(8,128)}, f32[3,5,2,16,128]{4,3,2,1,0:T(8,128)S(1)}, u32[]{:S(2)}) %copy-start.9) | copy-done | bytes 245784
  28.2 33.0 %shard_map.55 = f32[1,5,8,16,128]{4,3,2,1,0:T(8,128)} custom-call(f32[5,8,16,128]{3,2,1,0:T(8,128)} %refs_0_.1, f32[3,5,2,16,128]{4,3,2,1,0:T(8,128)} %copy-done, f32[3,5,2,16,128]{4,3,2,1,0:T(8,128)} %copy-done.5, f32[3,5,2,16,128]{4,3,2,1,0:T(8,128)} %copy-done.4, f32[3,5,2,16,128]{4,3,2,1,0:T(8,128)} %copy-done.3, f32[5,8,16,128]{3,2,1,0:T(8,128)} %copy-done.2, ...), custom_call_target="tpu_custom_call" | custom-call | tf_op jit(solution)/shard_map/pallas_call | solution.py:284
  (21 shorter events, 0.1 us)
Async XLA Ops:
  0.0 13.7 %copy-start.1 = (f32[5,8,16,128]{3,2,1,0:T(8,128)S(1)}, f32[5,8,16,128]{3,2,1,0:T(8,128)}, u32[]{:S(2)}) copy-start(f32[5,8,16,128]{3,2,1,0:T(8,128)} %refs_0_.1) | copy-start | bytes 983044
  1.0 5.2 %collective-permute-start.2 = (f32[5,2,16,128]{3,2,1,0:T(8,128)S(1)}, f32[5,2,16,128]{3,2,1,0:T(8,128)S(1)}, u32[]{:S(2)}, u32[]{:S(2)}) collective-permute-start(f32[5,2,16,128]{3,2,1,0:T(8,128)S(1)} %constant_dynamic-slice_fusion), channel_id=1, source_target_pairs={{2,0},{4,2},{6,4},{0,6},{3,1},{5,3},{7,5},{1,7},{10,8},{12,10},{14... | collective-permute-start | bytes 245768 | tf_op jit(solution)/shard_map/ppermute | solution.py:303
  1.1 5.1 %collective-permute-start.1 = (f32[5,2,16,128]{3,2,1,0:T(8,128)S(1)}, f32[5,2,16,128]{3,2,1,0:T(8,128)S(1)}, u32[]{:S(2)}, u32[]{:S(2)}) collective-permute-start(f32[5,2,16,128]{3,2,1,0:T(8,128)S(1)} %constant_dynamic-slice_fusion), channel_id=1, source_target_pairs={{6,0},{0,2},{2,4},{4,6},{7,1},{1,3},{3,5},{5,7},{14,8},{8,10},{10,... | collective-permute-start | bytes 245768 | tf_op jit(solution)/shard_map/ppermute | solution.py:303
  4.2 6.7 %collective-permute-start = (f32[5,2,16,128]{3,2,1,0:T(8,128)S(1)}, f32[5,2,16,128]{3,2,1,0:T(8,128)S(1)}, u32[]{:S(2)}, u32[]{:S(2)}) collective-permute-start(f32[5,2,16,128]{3,2,1,0:T(8,128)S(1)} %constant_dynamic-slice_fusion), channel_id=1, source_target_pairs={{4,0},{6,2},{0,4},{2,6},{5,1},{7,3},{1,5},{3,7},{12,8},{14,10},{8,... | collective-permute-start | bytes 245768 | tf_op jit(solution)/shard_map/ppermute | solution.py:303
  11.0 16.1 %copy-start = (f32[3,5,2,16,128]{4,3,2,1,0:T(8,128)}, f32[3,5,2,16,128]{4,3,2,1,0:T(8,128)S(1)}, u32[]{:S(2)}) copy-start(f32[3,5,2,16,128]{4,3,2,1,0:T(8,128)S(1)} %pad_maximum_fusion.refs_1_) | copy-start | bytes 737284
  11.0 7.4 %collective-permute-start.5 = (f32[3,5,2,16,128]{4,3,2,1,0:T(8,128)S(1)}, f32[3,5,2,16,128]{4,3,2,1,0:T(8,128)S(1)}, u32[]{:S(2)}, u32[]{:S(2)}) collective-permute-start(f32[3,5,2,16,128]{4,3,2,1,0:T(8,128)S(1)} %pad_maximum_fusion.refs_1_), channel_id=1, source_target_pairs={{0,24},{8,16},{16,8},{24,0},{1,25},{9,17},{17,9},{25,1},{2,26},{10... | collective-permute-start | bytes 737288 | tf_op jit(solution)/shard_map/ppermute | solution.py:307
  12.2 12.9 %collective-permute-start.4 = (f32[3,5,2,16,128]{4,3,2,1,0:T(8,128)S(1)}, f32[3,5,2,16,128]{4,3,2,1,0:T(8,128)S(1)}, u32[]{:S(2)}, u32[]{:S(2)}) collective-permute-start(f32[3,5,2,16,128]{4,3,2,1,0:T(8,128)S(1)} %pad_maximum_fusion.refs_1_), channel_id=1, source_target_pairs={{0,16},{8,24},{16,0},{24,8},{1,17},{9,25},{17,1},{25,9},{2,18},{10... | collective-permute-start | bytes 737288 | tf_op jit(solution)/shard_map/ppermute | solution.py:307
  13.5 12.1 %collective-permute-start.3 = (f32[3,5,2,16,128]{4,3,2,1,0:T(8,128)S(1)}, f32[3,5,2,16,128]{4,3,2,1,0:T(8,128)S(1)}, u32[]{:S(2)}, u32[]{:S(2)}) collective-permute-start(f32[3,5,2,16,128]{4,3,2,1,0:T(8,128)S(1)} %pad_maximum_fusion.refs_1_), channel_id=1, source_target_pairs={{0,8},{8,0},{16,24},{24,16},{1,9},{9,1},{17,25},{25,17},{2,10},{10... | collective-permute-start | bytes 737288 | tf_op jit(solution)/shard_map/ppermute | solution.py:307
  13.7 12.0 %collective-permute-start.6 = (f32[5,8,16,128]{3,2,1,0:T(8,128)S(1)}, f32[5,8,16,128]{3,2,1,0:T(8,128)S(1)}, u32[]{:S(2)}, u32[]{:S(2)}) collective-permute-start(f32[5,8,16,128]{3,2,1,0:T(8,128)S(1)} %copy-done.1), channel_id=1, source_target_pairs={{0,1},{1,0},{2,3},{3,2},{4,5},{5,4},{6,7},{7,6},{8,9},{9,8},{10,11... | collective-permute-start | bytes 983048 | tf_op jit(solution)/shard_map/ppermute | solution.py:300
  15.6 10.1 %collective-permute-start.7 = (f32[3,5,2,16,128]{4,3,2,1,0:T(8,128)S(1)}, f32[3,5,2,16,128]{4,3,2,1,0:T(8,128)S(1)}, u32[]{:S(2)}, u32[]{:S(2)}) collective-permute-start(f32[3,5,2,16,128]{4,3,2,1,0:T(8,128)S(1)} %pad_maximum_fusion.refs_1_), channel_id=1, source_target_pairs={{0,1},{1,0},{2,3},{3,2},{4,5},{5,4},{6,7},{7,6},{8,9},{9,8},{10,11... | collective-permute-start | bytes 737288 | tf_op jit(solution)/shard_map/ppermute | solution.py:308
  18.4 8.7 %copy-start.3 = (f32[3,5,2,16,128]{4,3,2,1,0:T(8,128)}, f32[3,5,2,16,128]{4,3,2,1,0:T(8,128)S(1)}, u32[]{:S(2)}) copy-start(f32[3,5,2,16,128]{4,3,2,1,0:T(8,128)S(1)} %collective-permute-done.5.refs_4_) | copy-start | bytes 737284
  18.4 7.3 %collective-permute-start.10 = (f32[3,5,2,16,128]{4,3,2,1,0:T(8,128)S(1)}, f32[3,5,2,16,128]{4,3,2,1,0:T(8,128)S(1)}, u32[]{:S(2)}, u32[]{:S(2)}) collective-permute-start(f32[3,5,2,16,128]{4,3,2,1,0:T(8,128)S(1)} %collective-permute-done.5.refs_4_), channel_id=1, source_target_pairs={{0,1},{1,0},{2,3},{3,2},{4,5},{5,4},{6,7},{7,6},{8,9},{9,8},{10,11... | collective-permute-start | bytes 737288 | tf_op jit(solution)/shard_map/ppermute | solution.py:308
  25.1 2.0 %copy-start.4 = (f32[3,5,2,16,128]{4,3,2,1,0:T(8,128)}, f32[3,5,2,16,128]{4,3,2,1,0:T(8,128)S(1)}, u32[]{:S(2)}) copy-start(f32[3,5,2,16,128]{4,3,2,1,0:T(8,128)S(1)} %collective-permute-done.4.refs_3_) | copy-start | bytes 737284
  25.1 1.6 %collective-permute-start.9 = (f32[3,5,2,16,128]{4,3,2,1,0:T(8,128)S(1)}, f32[3,5,2,16,128]{4,3,2,1,0:T(8,128)S(1)}, u32[]{:S(2)}, u32[]{:S(2)}) collective-permute-start(f32[3,5,2,16,128]{4,3,2,1,0:T(8,128)S(1)} %collective-permute-done.4.refs_3_), channel_id=1, source_target_pairs={{0,1},{1,0},{2,3},{3,2},{4,5},{5,4},{6,7},{7,6},{8,9},{9,8},{10,11... | collective-permute-start | bytes 737288 | tf_op jit(solution)/shard_map/ppermute | solution.py:308
  25.6 1.5 %copy-start.5 = (f32[3,5,2,16,128]{4,3,2,1,0:T(8,128)}, f32[3,5,2,16,128]{4,3,2,1,0:T(8,128)S(1)}, u32[]{:S(2)}) copy-start(f32[3,5,2,16,128]{4,3,2,1,0:T(8,128)S(1)} %collective-permute-done.3.refs_2_) | copy-start | bytes 737284
  25.6 1.5 %collective-permute-start.8 = (f32[3,5,2,16,128]{4,3,2,1,0:T(8,128)S(1)}, f32[3,5,2,16,128]{4,3,2,1,0:T(8,128)S(1)}, u32[]{:S(2)}, u32[]{:S(2)}) collective-permute-start(f32[3,5,2,16,128]{4,3,2,1,0:T(8,128)S(1)} %collective-permute-done.3.refs_2_), channel_id=1, source_target_pairs={{0,1},{1,0},{2,3},{3,2},{4,5},{5,4},{6,7},{7,6},{8,9},{9,8},{10,11... | collective-permute-start | bytes 737288 | tf_op jit(solution)/shard_map/ppermute | solution.py:308
  25.7 1.5 %copy-start.6 = (f32[3,5,2,16,128]{4,3,2,1,0:T(8,128)}, f32[3,5,2,16,128]{4,3,2,1,0:T(8,128)S(1)}, u32[]{:S(2)}) copy-start(f32[3,5,2,16,128]{4,3,2,1,0:T(8,128)S(1)} %collective-permute-done.7.refs_6_) | copy-start | bytes 737284
  25.7 1.5 %copy-start.2 = (f32[5,8,16,128]{3,2,1,0:T(8,128)}, f32[5,8,16,128]{3,2,1,0:T(8,128)S(1)}, u32[]{:S(2)}) copy-start(f32[5,8,16,128]{3,2,1,0:T(8,128)S(1)} %collective-permute-done.6.refs_5_) | copy-start | bytes 983044
  25.7 1.4 %copy-start.7 = (f32[3,5,2,16,128]{4,3,2,1,0:T(8,128)}, f32[3,5,2,16,128]{4,3,2,1,0:T(8,128)S(1)}, u32[]{:S(2)}) copy-start(f32[3,5,2,16,128]{4,3,2,1,0:T(8,128)S(1)} %collective-permute-done.10.refs_9_) | copy-start | bytes 737284
  26.7 0.7 %copy-start.8 = (f32[3,5,2,16,128]{4,3,2,1,0:T(8,128)}, f32[3,5,2,16,128]{4,3,2,1,0:T(8,128)S(1)}, u32[]{:S(2)}) copy-start(f32[3,5,2,16,128]{4,3,2,1,0:T(8,128)S(1)} %collective-permute-done.9.refs_8_) | copy-start | bytes 737284
  27.5 0.7 %copy-start.9 = (f32[3,5,2,16,128]{4,3,2,1,0:T(8,128)}, f32[3,5,2,16,128]{4,3,2,1,0:T(8,128)S(1)}, u32[]{:S(2)}) copy-start(f32[3,5,2,16,128]{4,3,2,1,0:T(8,128)S(1)} %collective-permute-done.8.refs_7_) | copy-start | bytes 737284
